TPU v7x, 256 devices: a whole 4x4x8 slice. The times are simulated.
256 devices in a mesh: blk: 8 (over x, core), row: 32 (over z, y).
Axes of the slice: x: 4, y: 4, z: 8, core: 2. Of those that a mesh axis runs over, the one named last changes fastest.
Arguments:
- dyn_state: float32 [4, 72, 128, 256], P(None, None, 'blk', 'row'), may hold values from -6 to 6
- crm_state: bfloat16 [3, 58, 524288], P(None, None, ('blk', 'row')), may hold values from -6 to 6
- cloud_mask: int32 [58, 524288], P(None, ('blk', 'row')), may hold values 0 or 1
- span_of: int32 [8192, 1], P(('blk', 'row')), may hold values from 0 to 31; in each aligned block of 32 rows (0 to 31, 32 to 63, ...) at most 2 rows name the same one
Outputs:
- dyn_out: float32 [4, 72, 128, 256], P(None, None, 'blk', 'row')
- crm_out: bfloat16 [3, 58, 524288], P(None, None, ('blk', 'row'))
Inputs may be any that keep to these rules, and one draw needn't show every extreme that they name: `span_of`: within the 32 columns of one device at most 2 name the same span, a bound that some block reaches.
All inputs are finite; a program needn't handle non-finite values. No bound on the sum of `cloud_mask` on one device may be relied on, other than what follows from the above.
Results may differ from a plain program's by a relative error of at most 0.001.
Values sent between devices are 32-bit elements; how exact they have to be, the bound alone decides.
A program may use at most 128 MiB of HBM per device.

v0:
```python
import jax
import jax.numpy as jnp
import numpy as np
from jax import lax
from jax.sharding import PartitionSpec as P

CRM_COLS = 32
SUBSTEPS = 2


def with_halo(block, sides, width):
    for axis, dim in sides:
        count = lax.axis_size(axis)
        forward = [(i, i + 1) for i in range(count - 1)]
        forward.append((count - 1, 0))
        backward = [(target, source) for source, target in forward]
        low = lax.ppermute(
            lax.slice_in_dim(block, block.shape[dim] - width, None, axis=dim), axis, forward
        )
        high = lax.ppermute(lax.slice_in_dim(block, 0, width, axis=dim), axis, backward)
        block = jnp.concatenate([low, block, high], axis=dim)
    return block


def poly_times(first_poly, second_poly):
    product = [0.0] * (len(first_poly) + len(second_poly) - 1)
    for first_index in range(len(first_poly)):
        for second_index in range(len(second_poly)):
            product[first_index + second_index] += (
                first_poly[first_index] * second_poly[second_index]
            )
    return product


def poly_slope(coeffs, point):
    result_value = 0.0
    for power in range(1, len(coeffs)):
        result_value += power * coeffs[power] * point ** (power - 1)
    return result_value


def poly_integral(coeffs, lower_end, upper_end):
    result_value = 0.0
    for power in range(len(coeffs)):
        result_value += (
            coeffs[power] * (upper_end ** (power + 1) - lower_end ** (power + 1)) / (power + 1)
        )
    return result_value


def element_tables():
    root_five = float(np.sqrt(5.0))
    gll_nodes = [-1.0, -1.0 / root_five, 1.0 / root_five, 1.0]
    weights = np.array([1.0 / 6.0, 5.0 / 6.0, 5.0 / 6.0, 1.0 / 6.0])
    derivative = np.zeros((4, 4))
    to_cells = np.zeros((2, 4))
    for basis in range(4):
        coeffs = [1.0]
        for other in range(4):
            if other != basis:
                denominator = gll_nodes[basis] - gll_nodes[other]
                coeffs = poly_times(coeffs, [-gll_nodes[other] / denominator, 1.0 / denominator])
        for node in range(4):
            derivative[node, basis] = poly_slope(coeffs, gll_nodes[node])
        to_cells[0, basis] = poly_integral(coeffs, -1.0, 0.0)
        to_cells[1, basis] = poly_integral(coeffs, 0.0, 1.0)
    to_nodes = np.array([[1.0, 0.0], [1.0, 0.0], [0.0, 1.0], [0.0, 1.0]])
    edge_weights = np.array([1.0 / 3.0, 5.0 / 6.0, 5.0 / 6.0, 1.0 / 3.0])
    return (derivative, weights, to_cells, to_nodes, edge_weights)


def slot_mean(field, ncols):
    return field.reshape(field.shape[0], -1, ncols).mean(axis=2)


def spread(profile, ncols):
    return jnp.repeat(profile, ncols, axis=1)


def transport(field, momentum, ncols):
    column = lax.broadcasted_iota(jnp.int32, field.shape, 1) % ncols
    east = jnp.where(
        column == ncols - 1, jnp.roll(field, ncols - 1, axis=1), jnp.roll(field, -1, axis=1)
    )
    west = jnp.where(column == 0, jnp.roll(field, 1 - ncols, axis=1), jnp.roll(field, 1, axis=1))
    upper = jnp.concatenate([field[1:], field[-1:]], axis=0)
    lower = jnp.concatenate([field[:1], field[:-1]], axis=0)
    return (
        field
        - 0.2 * momentum * (east - west) * 0.5
        + 0.15 * (east - 2.0 * field + west)
        + 0.15 * (upper - 2.0 * field + lower)
    )


def crm_substep(fields, forcing, wet, saturation, ncols):
    momentum = fields[2]
    moved = []
    for field, target in zip(fields, forcing):
        moved.append(
            transport(field, momentum, ncols)
            + 0.3 * spread(target - slot_mean(field, ncols), ncols)
        )
    heat, water, motion = moved
    condensed = wet * 0.5 * jnp.maximum(water - 0.5 * heat - saturation, 0.0)
    return (heat + 0.8 * condensed, water - condensed, motion)


def cloud_model(state, profiles, cloud_mask, ncols):
    levels = state.shape[1]
    start = tuple((state[k].astype(jnp.float32) for k in range(3)))
    forcing = tuple((profiles[k, :levels] for k in range(3)))
    wet = cloud_mask.astype(jnp.float32)
    saturation = (0.5 - jnp.arange(levels, dtype=jnp.float32) / levels)[:, None]
    fields = start
    for substep in range(SUBSTEPS):
        fields = crm_substep(fields, forcing, wet, saturation, ncols)
    final = jnp.stack(fields).astype(jnp.bfloat16)
    change = jnp.stack([slot_mean(fields[k] - start[k], ncols) for k in range(3)])
    tendency = jnp.pad(change, ((0, 0), (0, profiles.shape[1] - levels), (0, 0)))
    return (final, tendency)


def fold_first(padded):
    interior = padded[:, :, 1:-1]
    node_first = (jnp.arange(interior.shape[2]) % 4)[:, None]
    return (
        interior
        + jnp.where(node_first == 0, padded[:, :, :-2], 0.0)
        + jnp.where(node_first == 3, padded[:, :, 2:], 0.0)
    )


def fold_second(padded):
    interior = padded[..., 1:-1]
    node_along = jnp.arange(interior.shape[3]) % 4
    return (
        interior
        + jnp.where(node_along == 0, padded[..., :-2], 0.0)
        + jnp.where(node_along == 3, padded[..., 2:], 0.0)
    )


def edge_sum(field):
    padded = with_halo(field, (("blk", 2), ("row", 3)), 1)
    return fold_second(fold_first(padded))


def per_device(dyn_state, crm_state, cloud_mask, span_of):
    derivative, weights, to_cells, to_nodes, edge_weights = element_tables()
    highest = lax.Precision.HIGHEST
    levels = dyn_state.shape[1]
    first_count = dyn_state.shape[2] // 4
    elements = dyn_state.shape[3] // 4
    columns = span_of.shape[0]
    slots = 2 * columns
    spans = lax.axis_size("row")
    capacity = slots // spans
    derivative_x = jnp.asarray(np.kron(np.eye(first_count), derivative), jnp.float32)
    derivative_y = jnp.asarray(np.kron(np.eye(elements), derivative), jnp.float32)
    weight_x = jnp.asarray(np.tile(weights, first_count), jnp.float32)
    weight_y = jnp.asarray(np.tile(weights, elements), jnp.float32)
    mass = jnp.asarray(
        np.outer(np.tile(weights, first_count), np.tile(weights, elements)), jnp.float32
    )
    total = jnp.asarray(
        np.outer(np.tile(edge_weights, first_count), np.tile(edge_weights, elements)), jnp.float32
    )
    cell_x = jnp.asarray(np.kron(np.eye(first_count), to_cells), jnp.float32)
    cell_y = jnp.asarray(np.kron(np.eye(elements), to_cells.T), jnp.float32)
    node_x = jnp.asarray(np.kron(np.eye(first_count), to_nodes), jnp.float32)
    node_y = jnp.asarray(np.kron(np.eye(elements), to_nodes.T), jnp.float32)
    cells = jnp.einsum("ai,flij->flaj", cell_x, dyn_state[:3], precision=highest)
    cells = jnp.einsum("flaj,jc->flac", cells, cell_y, precision=highest).reshape(
        3, levels, columns
    )
    span_index = span_of[:, 0]
    match = (span_index[:, None] == jnp.arange(spans, dtype=jnp.int32)[None, :]).astype(jnp.int32)
    earlier = jnp.cumsum(match, axis=0) - match
    within = jnp.sum(earlier * match, axis=1)
    position = span_index * capacity + within
    place = (position[:, None] == jnp.arange(slots, dtype=jnp.int32)[None, :]).astype(jnp.float32)
    outgoing = jnp.einsum("flc,cp->flp", cells, place, precision=highest)
    arrived = lax.all_to_all(outgoing, "row", split_axis=2, concat_axis=2, tiled=True)
    crm_out, tendency = cloud_model(crm_state, arrived, cloud_mask, CRM_COLS)
    returned = lax.all_to_all(tendency, "row", split_axis=2, concat_axis=2, tiled=True)
    column_tendency = jnp.einsum("flp,cp->flc", returned, place, precision=highest)
    column_tendency = column_tendency.reshape(3, levels, 2 * first_count, 2 * elements)
    node_tendency = jnp.einsum("ia,flac->flic", node_x, column_tendency, precision=highest)
    node_tendency = jnp.einsum("flic,cy->fliy", node_tendency, node_y, precision=highest)
    raw = jnp.concatenate([dyn_state[:3] + node_tendency, dyn_state[3:]], axis=0)
    summed = edge_sum(mass * raw)
    state_one = summed / total
    gradient_x = jnp.einsum("km,flmy->flky", derivative_x, state_one, precision=highest)
    contrib = (
        -jnp.einsum("ki,k,flky->fliy", derivative_x, weight_x, gradient_x, precision=highest)
        * weight_y
    )
    gradient_y = jnp.einsum("fliy,ky->flik", state_one, derivative_y, precision=highest)
    contrib = (
        contrib
        - jnp.einsum("flik,ky->fliy", gradient_y * weight_y, derivative_y, precision=highest)
        * weight_x[:, None]
    )
    dyn_out = state_one + 0.01 * edge_sum(contrib) / total
    return (dyn_out, crm_out)


def solution(mesh):
    return jax.shard_map(
        per_device,
        mesh=mesh,
        in_specs=(
            P(None, None, "blk", "row"),
            P(None, None, ("blk", "row")),
            P(None, ("blk", "row")),
            P(("blk", "row"), None),
        ),
        out_specs=(P(None, None, "blk", "row"), P(None, None, ("blk", "row"))),
        check_vma=False,
    )
```

profile of v0, /device:TPU:1, one launch (start us, length us, event | category | flops | bytes accessed | tf_op | source)
XLA Modules:
  0.0 153.4 jit_solution(13753043464990080770)
XLA Ops:
  7.0 12.0 %all-to-all-start = ((f32[32,1,432]{2,1,0:T(1,128)}), f32[32,1,432]{2,1,0:T(1,128)S(1)}, u32[]{:S(2)}, u32[]{:S(2)}) async-start(f32[32,1,432]{2,1,0:T(1,128)} %reshape.945), calls=%async_computation | async-start | bytes 131072 | tf_op jit(solution)/shard_map/all_to_all | solution.py:184
  21.8 1.6 %copy-done.1 = f32[58,2048]{0,1:T(8,128)S(1)} copy-done((f32[58,2048]{0,1:T(8,128)S(1)}, f32[58,2048]{0,1:T(8,128)}, u32[]{:S(2)}) %copy-start.1) | copy-done | bytes 475160
  23.4 2.1 %fusion.122 = (f32[58,2047]{0,1:T(8,128)}, f32[58,2047]{0,1:T(8,128)}, f32[58,2047]{0,1:T(8,128)}, f32[58,2047]{0,1:T(8,128)}) fusion(f32[58,2048]{0,1:T(8,128)S(1)} %get-tuple-element.130, f32[58,2048]{0,1:T(8,128)S(1)} %copy-done.1), kind=kLoop, calls=%fused_computation.230 | loop fusion | bytes 3799232 | tf_op jit(solution)/shard_map/jit(_roll_static)/slice | solution.py:83
  25.4 2.1 %fusion.121 = (f32[58,2017]{0,1:T(8,128)}, f32[58,2017]{0,1:T(8,128)}, f32[58,2017]{0,1:T(8,128)}, f32[58,2017]{0,1:T(8,128)}) fusion(f32[58,2048]{0,1:T(8,128)S(1)} %get-tuple-element.130, f32[58,2048]{0,1:T(8,128)S(1)} %copy-done.1), kind=kLoop, calls=%fused_computation.229 | loop fusion | bytes 3743552 | tf_op jit(solution)/shard_map/jit(_roll_static)/slice | solution.py:83
  28.7 2.7 %slice_bitcast_fusion.3 = (f32[57,2048]{0,1:T(8,128)}, f32[57,2048]{0,1:T(8,128)}, f32[57,2048]{0,1:T(8,128)}, f32[57,2048]{0,1:T(8,128)}) fusion(f32[1,58,2048]{1,2,0:T(8,128)S(1)} %get-tuple-element.131, f32[1,58,2048]{1,2,0:T(8,128)S(1)} %get-tuple-element.133), kind=kLoop, calls=%fused_computation.37 | loop fusion | bytes 3735552 | tf_op jit(solution)/shard_map/slice | solution.py:86
  31.4 2.5 %slice_bitcast_fusion.2 = (f32[1,2048]{0,1:T(8,128)}, f32[1,2048]{0,1:T(8,128)}, f32[1,2048]{0,1:T(8,128)}, f32[1,2048]{0,1:T(8,128)}) fusion(f32[1,58,2048]{1,2,0:T(8,128)S(1)} %get-tuple-element.131, f32[1,58,2048]{1,2,0:T(8,128)S(1)} %get-tuple-element.133), kind=kLoop, calls=%fused_computation.36 | loop fusion | bytes 65536 | tf_op jit(solution)/shard_map/slice | solution.py:86
  35.9 2.3 %slice_bitcast_fusion.31 = (f32[1,58,2047]{1,2,0:T(8,128)}, f32[1,58,2047]{1,2,0:T(8,128)}, f32[58,2047]{0,1:T(8,128)}, f32[58,2047]{0,1:T(8,128)}) fusion(f32[58,2048]{0,1:T(8,128)S(1)} %get-tuple-element.128), kind=kLoop, calls=%fused_computation.214 | loop fusion | bytes 2849424 | tf_op jit(solution)/shard_map/jit(_roll_static)/concatenate | solution.py:83
  38.2 2.2 %slice_bitcast_fusion.19 = (f32[1,58,2017]{1,2,0:T(8,128)}, f32[1,58,2017]{1,2,0:T(8,128)}, f32[58,2017]{0,1:T(8,128)}, f32[58,2017]{0,1:T(8,128)}) fusion(f32[58,2048]{0,1:T(8,128)S(1)} %get-tuple-element.128), kind=kLoop, calls=%fused_computation.202 | loop fusion | bytes 2807664 | tf_op jit(solution)/shard_map/jit(_roll_static)/concatenate | solution.py:83
  41.6 1.7 %slice_bitcast_fusion.29 = (f32[57,2048]{0,1:T(8,128)}, f32[57,2048]{0,1:T(8,128)}) fusion(f32[1,58,2048]{1,2,0:T(8,128)S(1)} %get-tuple-element.129), kind=kLoop, calls=%fused_computation.212 | loop fusion | bytes 1867776 | tf_op jit(solution)/shard_map/slice | solution.py:86
  43.3 1.7 %slice_bitcast_fusion.28 = (f32[1,2048]{0,1:T(8,128)}, f32[1,2048]{0,1:T(8,128)}) fusion(f32[1,58,2048]{1,2,0:T(8,128)S(1)} %get-tuple-element.129), kind=kLoop, calls=%fused_computation.211 | loop fusion | bytes 32768 | tf_op jit(solution)/shard_map/slice | solution.py:86
  45.0 1.6 %fusion.129 = (f32[1,57,2048]{1,2,0:T(8,128)}, f32[1,57,2048]{1,2,0:T(8,128)}) fusion(bf16[1,58,2048]{1,2,0:T(8,128)(2,1)S(1)} %copy.196), kind=kLoop, calls=%fused_computation.237 | loop fusion | bytes 1867776 | tf_op jit(solution)/shard_map/slice | solution.py:86
  46.6 1.5 %fusion.130 = (f32[1,1,2048]{1,2,0:T(8,128)}, f32[1,1,2048]{1,2,0:T(8,128)}) fusion(bf16[1,58,2048]{1,2,0:T(8,128)(2,1)S(1)} %copy.196), kind=kLoop, calls=%fused_computation.238 | loop fusion | bytes 32768 | tf_op jit(solution)/shard_map/slice | solution.py:86
  49.6 2.0 %reduce_sum.95 = f32[58,64]{0,1:T(8,128)} reduce(f32[58,64,32]{0,2,1:T(8,128)} %bitcast.232, f32[]{:T(128)} %constant.123.clone.1), dimensions={2}, to_apply=%region_3.4 | reduce | flops 115072 | bytes 489988 | tf_op jit(solution)/shard_map/reduce_sum | solution.py:73
  58.1 9.2 %bitcast_reduce_fusion.3 = (f32[58,64]{0,1:T(8,128)S(1)}, f32[58,2048]{0,1:T(8,128)S(1)}, f32[58,2048]{0,1:T(8,128)S(1)}, f32[58,2048]{0,1:T(8,128)S(1)}) fusion(f32[58]{0:T(128)} %multiply_subtract_fusion, s32[58,2048]{0,1:T(8,128)S(1)} %copy.163, f32[58,64]{0,1:T(8,128)S(1)} %get-tuple-element.150, f32[57,2048]{0,1:T(8,128)} %get-tuple-element.147, ...), kind=kLoop, calls=%fused_computation.101 | loop fusion | flops 7242112 | bytes 8378088 | tf_op jit(solution)/shard_map/reduce_sum | solution.py:73
  68.7 1.5 %fusion.109 = (f32[58,2017]{0,1:T(8,128)}, f32[58,2017]{0,1:T(8,128)}) fusion(f32[58,2048]{0,1:T(8,128)S(1)} %get-tuple-element.26), kind=kLoop, calls=%fused_computation.217 | loop fusion | bytes 1871776 | tf_op jit(solution)/shard_map/jit(_roll_static)/slice | solution.py:83
  71.2 1.4 fusion.115
  75.0 9.9 %convert_bitcast_fusion.1 = (bf16[1,58,2048]{1,2,0:T(8,128)(2,1)}, f32[58,2048]{0,1:T(8,128)S(1)}, f32[58,2048]{0,1:T(8,128)S(1)}, f32[58,2048]{0,1:T(8,128)S(1)...) fusion(f32[58]{0:T(128)S(1)} %copy-done.40, ...), kind=kLoop, calls=%fused_computation.110 | loop fusion | flops 9740288 | bytes 14317288 | tf_op jit(solution)/shard_map/stack | solution.py:118
  84.9 1.7 %slice_bitcast_fusion.25 = (f32[1,58,2047]{1,2,0:T(8,128)}, f32[58,2047]{0,1:T(8,128)S(1)}, f32[58,2047]{0,1:T(8,128)S(1)}, f32[1,58,2047]{1,2,0:T(8,128)}) fusion(f32[58,2048]{0,1:T(8,128)S(1)} %get-tuple-element.14), kind=kLoop, calls=%fused_computation.208 | loop fusion | bytes 2849424 | tf_op jit(solution)/shard_map/jit(_roll_static)/concatenate | solution.py:83
  86.6 1.8 %slice_bitcast_fusion.21 = (f32[1,1,2048]{1,2,0:T(8,128)}, f32[1,1,2048]{1,2,0:T(8,128)}, f32[1,2048]{0,1:T(8,128)S(1)}, f32[1,2048]{0,1:T(8,128)S(1)}) fusion(f32[58,2048]{0,1:T(8,128)S(1)} %get-tuple-element.14), kind=kLoop, calls=%fused_computation.204 | loop fusion | bytes 49152 | tf_op jit(solution)/shard_map/concatenate | solution.py:87
  88.4 1.7 %slice_bitcast_fusion.20 = (f32[1,57,2048]{1,2,0:T(8,128)}, f32[1,57,2048]{1,2,0:T(8,128)}, f32[57,2048]{0,1:T(8,128)S(1)}, f32[57,2048]{0,1:T(8,128)S(1)}) fusion(f32[58,2048]{0,1:T(8,128)S(1)} %get-tuple-element.14), kind=kLoop, calls=%fused_computation.203 | loop fusion | bytes 2801664 | tf_op jit(solution)/shard_map/concatenate | solution.py:87
  90.1 1.5 slice_bitcast_fusion.17
  93.1 1.8 %fusion.106 = (f32[58,64]{0,1:T(8,128)S(1)}, f32[58,64,32]{0,2,1:T(8,128)S(1)}) fusion(f32[58,64]{0,1:T(8,128)S(1)} %subtract_multiply_fusion.3, f32[57,64,32]{0,2,1:T(8,128)S(1)} %bitcast.234, f32[1,64,32]{0,2,1:T(8,128)S(1)} %bitcast.236, f32[1,64,32]{0,2,1:T(8,128)S(1)} %bitcast.235, f32[57,64,32]{0,2,1:T(8,128)S(1)} %bitcast.233, ...), kind=kLoop, calls=%fused_computation.215 | loop fusion | flops 2728320 | bytes 3849216 | tf_op jit(solution)/shard_map/reduce_sum | solution.py:73
  96.3 2.7 %fusion.51 = f32[58,64]{0,1:T(8,128)S(1)} fusion(f32[58,64,32]{0,2,1:T(8,128)S(1)} %bitcast.230, f32[1,64,32]{0,2,1:T(8,128)S(1)} %bitcast.238, f32[57,64,32]{0,2,1:T(8,128)S(1)} %bitcast.240, f32[57,64,32]{0,2,1:T(8,128)S(1)} %bitcast.239, f32[1,64,32]{0,2,1:T(8,128)S(1)} %bitcast.237, f32[58,64,32]{0,2,1:T(8,128)S(1)} %get-tuple-element.28, ...), kind=kLoop, calls=%fused_computation.86 | loop fusion | flops 3322240 | bytes 3849216 | tf_op jit(solution)/shard_map/reduce_sum | solution.py:73
  100.3 9.2 %all-to-all-start.1 = ((f32[32,1,432]{2,1,0:T(1,128)}), f32[32,1,432]{2,1,0:T(1,128)S(1)}, u32[]{:S(2)}, u32[]{:S(2)}) async-start(f32[32,1,432]{2,1,0:T(1,128)} %reshape.947), calls=%async_computation.1 | async-start | bytes 131072 | tf_op jit(solution)/shard_map/all_to_all | solution.py:186
  109.6 8.8 %all-to-all-done.1 = f32[32,1,432]{2,1,0:T(1,128)S(1)} async-done(((f32[32,1,432]{2,1,0:T(1,128)}), f32[32,1,432]{2,1,0:T(1,128)S(1)}, u32[]{:S(2)}, u32[]{:S(2)}) %all-to-all-start.1) | async-done | bytes 55328 | tf_op jit(solution)/shard_map/all_to_all | solution.py:186
  120.5 3.8 %collective-permute-start = (f32[4,72,1,8]{1,2,3,0:T(1,128)S(1)}, f32[4,72,1,8]{1,2,3,0:T(1,128)S(1)}, u32[]{:S(2)}, u32[]{:S(2)}) collective-permute-start(f32[4,72,1,8]{1,2,3,0:T(1,128)S(1)} %get-tuple-element.140), channel_id=1, source_target_pairs={{0,32},{32,64},{64,96},{96,128},{128,160},{160,192},{192,224},{224... | collective-permute-start | bytes 27656 | tf_op jit(solution)/shard_map/ppermute | solution.py:17
  125.2 2.3 %collective-permute-done.1 = f32[4,72,1,8]{1,2,3,0:T(1,128)S(1)} collective-permute-done((f32[4,72,1,8]{1,2,3,0:T(1,128)S(1)}, f32[4,72,1,8]{1,2,3,0:T(1,128)S(1)}, u32[]{:S(2)}, u32[]{:S(2)}) %collective-permute-start.1) | collective-permute-done | bytes 9248 | tf_op jit(solution)/shard_map/ppermute | solution.py:20
  127.8 4.6 %collective-permute-start.3 = (f32[4,72,18,1]{1,2,3,0:T(8,128)S(1)}, f32[4,72,18,1]{1,2,3,0:T(8,128)S(1)}, u32[]{:S(2)}, u32[]{:S(2)}) collective-permute-start(f32[4,72,18,1]{1,2,3,0:T(8,128)S(1)} %get-tuple-element.137), channel_id=1, source_target_pairs={{1,0},{2,1},{3,2},{4,3},{5,4},{6,5},{7,6},{8,7},{9,8},{10,9},{11,1... | collective-permute-start | bytes 62216 | tf_op jit(solution)/shard_map/ppermute | solution.py:20
  132.4 1.5 collective-permute-done.2
  137.5 7.0 %fusion.60 = bf16[1,58,2048]{1,2,0:T(8,128)(2,1)S(1)} fusion(f32[1,1,2048]{1,2,0:T(8,128)} %get-tuple-element.62, f32[1,57,2048]{1,2,0:T(8,128)} %get-tuple-element.66, f32[1,57,2048]{1,2,0:T(8,128)} %get-tuple-element.65, f32[1,1,2048]{1,2,0:T(8,128)} %get-tuple-element.61, f32[1,58,2047]{1,2,0:T(8,128)} %get-tuple-element.56, ...), kind=kLoop, calls=%fused_computation.97 | loop fusion | flops 6057984 | bytes 6224896 | tf_op jit(solution)/shard_map/convert.5
  144.6 5.2 %collective-permute-start.7 = (f32[4,72,18,1]{1,2,3,0:T(8,128)S(1)}, f32[4,72,18,1]{1,2,3,0:T(8,128)S(1)}, u32[]{:S(2)}, u32[]{:S(2)}) collective-permute-start(f32[4,72,18,1]{1,2,3,0:T(8,128)S(1)} %get-tuple-element.135), channel_id=1, source_target_pairs={{1,0},{2,1},{3,2},{4,3},{5,4},{6,5},{7,6},{8,7},{9,8},{10,9},{11,1... | collective-permute-start | bytes 62216 | tf_op jit(solution)/shard_map/ppermute | solution.py:20
  150.2 1.5 copy.183
  (208 shorter events, 38.5 us)
Async XLA Ops:
  0.6 18.4 %copy-start.25 = (bf16[3,58,2048]{2,1,0:T(8,128)(2,1)S(1)}, bf16[3,58,2048]{2,1,0:T(8,128)(2,1)}, u32[]{:S(2)}) copy-start(bf16[3,58,2048]{2,1,0:T(8,128)(2,1)} %param.15) | copy-start | bytes 2138116
  7.0 47.4 %all-to-all-start = ((f32[32,1,432]{2,1,0:T(1,128)}), f32[32,1,432]{2,1,0:T(1,128)S(1)}, u32[]{:S(2)}, u32[]{:S(2)}) async-start(f32[32,1,432]{2,1,0:T(1,128)} %reshape.945), calls=%async_computation | async-start | bytes 131072 | tf_op jit(solution)/shard_map/all_to_all | solution.py:184
  99.0 20.2 %copy-start.51 = (s32[32]{0:T(128)S(1)}, s32[32]{0:T(128)}, u32[]{:S(2)}) copy-start(s32[32]{0:T(128)} %copy-done.50) | copy-start | bytes 388
  99.0 20.5 %copy-start.42 = (f32[16,8,1,1]{0,1,3,2:T(8,128)S(1)}, f32[16,8,1,1]{0,1,3,2:T(8,128)}, u32[]{:S(2)}) copy-start(f32[16,8,1,1]{0,1,3,2:T(8,128)} %constant.149) | copy-start | bytes 1540
  99.0 20.8 %copy-start.47 = (f32[4,8,1,1]{1,0,3,2:T(4,128)S(1)}, f32[4,8,1,1]{1,0,3,2:T(4,128)}, u32[]{:S(2)}) copy-start(f32[4,8,1,1]{1,0,3,2:T(4,128)} %constant.150) | copy-start | bytes 388
  99.3 21.1 %copy-start.41 = (f32[16,8]{0,1:T(8,128)S(1)}, f32[16,8]{0,1:T(8,128)}, u32[]{:S(2)}) copy-start(f32[16,8]{0,1:T(8,128)} %constant.135.clone) | copy-start | bytes 1540
  100.3 18.0 %all-to-all-start.1 = ((f32[32,1,432]{2,1,0:T(1,128)}), f32[32,1,432]{2,1,0:T(1,128)S(1)}, u32[]{:S(2)}, u32[]{:S(2)}) async-start(f32[32,1,432]{2,1,0:T(1,128)} %reshape.947), calls=%async_computation.1 | async-start | bytes 131072 | tf_op jit(solution)/shard_map/all_to_all | solution.py:186
  119.5 17.8 %copy-start.30 = (f32[1,58,31]{1,2,0:T(8,128)S(1)}, f32[1,58,31]{1,2,0:T(8,128)}, u32[]{:S(2)}) copy-start(f32[1,58,31]{1,2,0:T(8,128)} %get-tuple-element.45) | copy-start | bytes 21580
  119.5 17.8 %copy-start.31 = (f32[1,58,31]{1,2,0:T(8,128)S(1)}, f32[1,58,31]{1,2,0:T(8,128)}, u32[]{:S(2)}) copy-start(f32[1,58,31]{1,2,0:T(8,128)} %get-tuple-element.46) | copy-start | bytes 21580
  119.5 17.8 %copy-start.45 = (f32[1,58,1]{1,2,0:T(1,128)S(1)}, f32[1,58,1]{1,2,0:T(1,128)}, u32[]{:S(2)}) copy-start(f32[1,58,1]{1,2,0:T(1,128)} %get-tuple-element.57) | copy-start | bytes 700
  119.5 17.8 %copy-start.46 = (f32[1,58,1]{1,2,0:T(1,128)S(1)}, f32[1,58,1]{1,2,0:T(1,128)}, u32[]{:S(2)}) copy-start(f32[1,58,1]{1,2,0:T(1,128)} %get-tuple-element.58) | copy-start | bytes 700
  119.8 14.3 %copy-start.37 = (f32[16,8]{0,1:T(8,128)S(1)}, f32[16,8]{0,1:T(8,128)}, u32[]{:S(2)}) copy-start(f32[16,8]{0,1:T(8,128)} %constant.145) | copy-start | bytes 1540
  119.9 14.4 %copy-start.39 = (f32[8,8,1,1]{1,0,3,2:T(8,128)S(1)}, f32[8,8,1,1]{1,0,3,2:T(8,128)}, u32[]{:S(2)}) copy-start(f32[8,8,1,1]{1,0,3,2:T(8,128)} %constant.152) | copy-start | bytes 772
  119.9 14.4 %copy-start.48 = (f32[8]{0:T(128)S(1)}, f32[8]{0:T(128)}, u32[]{:S(2)}) copy-start(f32[8]{0:T(128)} %constant.134.clone) | copy-start | bytes 100
  119.9 15.3 %copy-start.34 = (f32[16,16,1,1]{1,0,3,2:T(8,128)S(1)}, f32[16,16,1,1]{1,0,3,2:T(8,128)}, u32[]{:S(2)}) copy-start(f32[16,16,1,1]{1,0,3,2:T(8,128)} %constant.151) | copy-start | bytes 3076
  119.9 15.3 %copy-start.49 = (f32[16]{0:T(128)S(1)}, f32[16]{0:T(128)}, u32[]{:S(2)}) copy-start(f32[16]{0:T(128)} %constant.133.clone) | copy-start | bytes 196
  119.9 17.4 %copy-start.28 = (f32[1,58,31]{1,2,0:T(8,128)S(1)}, f32[1,58,31]{1,2,0:T(8,128)}, u32[]{:S(2)}) copy-start(f32[1,58,31]{1,2,0:T(8,128)} %get-tuple-element.29) | copy-start | bytes 21580
  119.9 17.4 %copy-start.29 = (f32[1,58,31]{1,2,0:T(8,128)S(1)}, f32[1,58,31]{1,2,0:T(8,128)}, u32[]{:S(2)}) copy-start(f32[1,58,31]{1,2,0:T(8,128)} %get-tuple-element.30) | copy-start | bytes 21580
  119.9 17.4 %copy-start.36 = (pred[2048]{0:T(1024)(128)(4,1)S(1)}, pred[2048]{0:T(1024)(128)(4,1)}, u32[]{:S(2)}) copy-start(pred[2048]{0:T(1024)(128)(4,1)} %fusion.97) | copy-start | bytes 6148
  119.9 17.4 %copy-start.44 = (f32[1,58,1]{1,2,0:T(1,128)S(1)}, f32[1,58,1]{1,2,0:T(1,128)}, u32[]{:S(2)}) copy-start(f32[1,58,1]{1,2,0:T(1,128)} %get-tuple-element.42) | copy-start | bytes 700
  120.3 17.1 %copy-start.14 = (f32[1,58,2047]{1,2,0:T(8,128)S(1)}, f32[1,58,2047]{1,2,0:T(8,128)}, u32[]{:S(2)}) copy-start(f32[1,58,2047]{1,2,0:T(8,128)} %get-tuple-element.53) | copy-start | bytes 1424716
  120.4 17.0 %copy-start.12 = (f32[1,58,2047]{1,2,0:T(8,128)S(1)}, f32[1,58,2047]{1,2,0:T(8,128)}, u32[]{:S(2)}) copy-start(f32[1,58,2047]{1,2,0:T(8,128)} %get-tuple-element.37) | copy-start | bytes 1424716
  120.4 17.0 %copy-start.13 = (f32[1,58,2047]{1,2,0:T(8,128)S(1)}, f32[1,58,2047]{1,2,0:T(8,128)}, u32[]{:S(2)}) copy-start(f32[1,58,2047]{1,2,0:T(8,128)} %get-tuple-element.38) | copy-start | bytes 1424716
  120.5 4.7 %collective-permute-start = (f32[4,72,1,8]{1,2,3,0:T(1,128)S(1)}, f32[4,72,1,8]{1,2,3,0:T(1,128)S(1)}, u32[]{:S(2)}, u32[]{:S(2)}) collective-permute-start(f32[4,72,1,8]{1,2,3,0:T(1,128)S(1)} %get-tuple-element.140), channel_id=1, source_target_pairs={{0,32},{32,64},{64,96},{96,128},{128,160},{160,192},{192,224},{224... | collective-permute-start | bytes 27656 | tf_op jit(solution)/shard_map/ppermute | solution.py:17
  124.3 3.2 %collective-permute-start.1 = (f32[4,72,1,8]{1,2,3,0:T(1,128)S(1)}, f32[4,72,1,8]{1,2,3,0:T(1,128)S(1)}, u32[]{:S(2)}, u32[]{:S(2)}) collective-permute-start(f32[4,72,1,8]{1,2,3,0:T(1,128)S(1)} %get-tuple-element.141), channel_id=1, source_target_pairs={{32,0},{64,32},{96,64},{128,96},{160,128},{192,160},{224,192},{0,2... | collective-permute-start | bytes 27656 | tf_op jit(solution)/shard_map/ppermute | solution.py:20
  127.5 6.3 %collective-permute-start.2 = (f32[4,72,18,1]{1,2,3,0:T(8,128)S(1)}, f32[4,72,18,1]{1,2,3,0:T(8,128)S(1)}, u32[]{:S(2)}, u32[]{:S(2)}) collective-permute-start(f32[4,72,18,1]{1,2,3,0:T(8,128)S(1)} %get-tuple-element.136), channel_id=1, source_target_pairs={{0,1},{1,2},{2,3},{3,4},{4,5},{5,6},{6,7},{7,8},{8,9},{9,10},{10,1... | collective-permute-start | bytes 62216 | tf_op jit(solution)/shard_map/ppermute | solution.py:17
  127.8 6.0 %collective-permute-start.3 = (f32[4,72,18,1]{1,2,3,0:T(8,128)S(1)}, f32[4,72,18,1]{1,2,3,0:T(8,128)S(1)}, u32[]{:S(2)}, u32[]{:S(2)}) collective-permute-start(f32[4,72,18,1]{1,2,3,0:T(8,128)S(1)} %get-tuple-element.137), channel_id=1, source_target_pairs={{1,0},{2,1},{3,2},{4,3},{5,4},{6,5},{7,6},{8,7},{9,8},{10,9},{11,1... | collective-permute-start | bytes 62216 | tf_op jit(solution)/shard_map/ppermute | solution.py:20
  136.0 8.5 %collective-permute-start.4 = (f32[4,72,1,8]{1,2,3,0:T(1,128)S(1)}, f32[4,72,1,8]{1,2,3,0:T(1,128)S(1)}, u32[]{:S(2)}, u32[]{:S(2)}) collective-permute-start(f32[4,72,1,8]{1,2,3,0:T(1,128)S(1)} %get-tuple-element.138), channel_id=1, source_target_pairs={{0,32},{32,64},{64,96},{96,128},{128,160},{160,192},{192,224},{224... | collective-permute-start | bytes 27656 | tf_op jit(solution)/shard_map/ppermute | solution.py:17
  137.2 7.3 %collective-permute-start.5 = (f32[4,72,1,8]{1,2,3,0:T(1,128)S(1)}, f32[4,72,1,8]{1,2,3,0:T(1,128)S(1)}, u32[]{:S(2)}, u32[]{:S(2)}) collective-permute-start(f32[4,72,1,8]{1,2,3,0:T(1,128)S(1)} %get-tuple-element.139), channel_id=1, source_target_pairs={{32,0},{64,32},{96,64},{128,96},{160,128},{192,160},{224,192},{0,2... | collective-permute-start | bytes 27656 | tf_op jit(solution)/shard_map/ppermute | solution.py:20
  137.5 12.3 %copy-start.23 = (bf16[1,58,2048]{1,2,0:T(8,128)(2,1)S(1)}, bf16[1,58,2048]{1,2,0:T(8,128)(2,1)}, u32[]{:S(2)}) copy-start(bf16[1,58,2048]{1,2,0:T(8,128)(2,1)} %get-tuple-element.19) | copy-start | bytes 712708
  144.5 7.2 %collective-permute-start.6 = (f32[4,72,18,1]{1,2,3,0:T(8,128)S(1)}, f32[4,72,18,1]{1,2,3,0:T(8,128)S(1)}, u32[]{:S(2)}, u32[]{:S(2)}) collective-permute-start(f32[4,72,18,1]{1,2,3,0:T(8,128)S(1)} %get-tuple-element.134), channel_id=1, source_target_pairs={{0,1},{1,2},{2,3},{3,4},{4,5},{5,6},{6,7},{7,8},{8,9},{9,10},{10,1... | collective-permute-start | bytes 62216 | tf_op jit(solution)/shard_map/ppermute | solution.py:17
  144.6 7.1 %collective-permute-start.7 = (f32[4,72,18,1]{1,2,3,0:T(8,128)S(1)}, f32[4,72,18,1]{1,2,3,0:T(8,128)S(1)}, u32[]{:S(2)}, u32[]{:S(2)}) collective-permute-start(f32[4,72,18,1]{1,2,3,0:T(8,128)S(1)} %get-tuple-element.135), channel_id=1, source_target_pairs={{1,0},{2,1},{3,2},{4,3},{5,4},{6,5},{7,6},{8,7},{9,8},{10,9},{11,1... | collective-permute-start | bytes 62216 | tf_op jit(solution)/shard_map/ppermute | solution.py:20
  (33 other events, 126.8 us)
where the time goes:
time: 154 us; the launch traced here: 153 us
  local copies, waits for them, and re-layouts  51 us (33%)
  other arithmetic  46.2 us (30%)
  starting transfers between devices  36.5 us (24%)
  waiting for transfers between devices  13.4 us (9%)
  matrix products  4.59 us (3%)
  between operations  1.71 us (1%)
    reduce_sum x9, other arithmetic, slot_mean(): return field.reshape(field.shape[0], -1, ncols).mean(axis=2)  18.4 us
    unnamed x121, local copies, waits for them, and re-layouts  13.2 us
    slice x10, local copies, waits for them, and re-layouts, transport(): upper = jnp.concatenate([field[1:], field[-1:]], axis=0)  13.1 us
    all_to_all x1, starting transfers between devices, per_device(): lax.all_to_all(outgoing, 'row', split_axis=2, concat_axis=2, tiled=True)  12 us
    another operation x3, other arithmetic, cloud_model(): final = jnp.stack(fields).astype(jnp.bfloat16)  11.4 us
    ppermute x4, starting transfers between devices, with_halo(): lax.ppermute(lax.slice_in_dim(block, 0, width, axis=dim), axis, backward)  9.93 us
    all_to_all x1, starting transfers between devices, per_device(): lax.all_to_all(tendency, 'row', split_axis=2, concat_axis=2, tiled=True)  9.22 us
    all_to_all x1, waiting for transfers between devices, per_device(): lax.all_to_all(tendency, 'row', split_axis=2, concat_axis=2, tiled=True)  8.79 us
  transfers between devices with their start and end apart: 10, of which 4 were waited for; matrix products, arithmetic and copies ran while one was open for 28% of the time, Pallas kernels for 0%

commit v1 on v0

v1 whole, which is shorter than its diff:
```python
import functools

import jax
import jax.numpy as jnp
import numpy as np
from jax import lax
from jax.experimental import pallas as pl
from jax.experimental.pallas import tpu as pltpu
from jax.sharding import PartitionSpec as P

MESH = pl.DeviceIdType.MESH
LEV, CRM_LEV, CRM_COLS = 72, 58, 32
F32, BF16 = jnp.float32, jnp.bfloat16
SLOTS = ((0, -1), (0, 1), (-1, 0), (1, 0), (-1, -1), (-1, 1), (1, -1), (1, 1))
STATE_ROWS = (32, 32, 16, 16, 8, 8, 8, 8)
CELL_ROWS = (24, 24, 16, 16, 8, 8, 8, 8)
STATE_AT = tuple(int(v) for v in np.cumsum((0,) + STATE_ROWS))
CELL_AT = tuple(int(v) for v in np.cumsum((0,) + CELL_ROWS))
HALO = CELL_AT[-1]
CELLS = 32 + HALO


def poly_times(first_poly, second_poly):
    product = [0.0] * (len(first_poly) + len(second_poly) - 1)
    for i, first in enumerate(first_poly):
        for j, second in enumerate(second_poly):
            product[i + j] += first * second
    return product


def poly_slope(coeffs, point):
    return sum(power * coeffs[power] * point ** (power - 1) for power in range(1, len(coeffs)))


def poly_integral(coeffs, low, high):
    return sum(
        coeffs[power] * (high ** (power + 1) - low ** (power + 1)) / (power + 1)
        for power in range(len(coeffs))
    )


def element_tables():
    root_five = float(np.sqrt(5.0))
    gll_nodes = [-1.0, -1.0 / root_five, 1.0 / root_five, 1.0]
    weights = np.array([1.0 / 6.0, 5.0 / 6.0, 5.0 / 6.0, 1.0 / 6.0])
    derivative = np.zeros((4, 4))
    to_cells = np.zeros((2, 4))
    for basis in range(4):
        coeffs = [1.0]
        for other in range(4):
            if other != basis:
                denominator = gll_nodes[basis] - gll_nodes[other]
                coeffs = poly_times(coeffs, [-gll_nodes[other] / denominator, 1.0 / denominator])
        for node in range(4):
            derivative[node, basis] = poly_slope(coeffs, gll_nodes[node])
        to_cells[0, basis] = poly_integral(coeffs, -1.0, 0.0)
        to_cells[1, basis] = poly_integral(coeffs, 0.0, 1.0)
    to_nodes = np.array([[1.0, 0.0], [1.0, 0.0], [0.0, 1.0], [0.0, 1.0]])
    edge_weights = np.array([1.0 / 3.0, 5.0 / 6.0, 5.0 / 6.0, 1.0 / 3.0])
    return derivative, weights, to_cells, to_nodes, edge_weights


def line_operators(elements):
    derivative, weights, _, _, edge_weights = element_tables()
    count = elements * 4 * 3
    weight = np.tile(weights, elements * 3)
    fold = np.eye(count)
    for node in range(count):
        if node % 4 == 0:
            fold[node, (node - 1) % count] += 1.0
        if node % 4 == 3:
            fold[node, (node + 1) % count] += 1.0
    fold = fold / np.tile(edge_weights, elements * 3)[:, None]
    smooth = fold * weight
    stiff = np.kron(np.eye(elements * 3), derivative.T @ np.diag(weights) @ derivative)
    mine = slice(elements * 4, elements * 8)
    return smooth[mine], (fold @ stiff @ smooth)[mine], (smooth @ smooth)[mine]


def split(value):
    high = np.asarray(value, np.float32).astype(jnp.bfloat16)
    return high, (np.asarray(value, np.float32) - high.astype(np.float32)).astype(jnp.bfloat16)


@functools.cache
def tables():
    _, _, to_cells, to_nodes, _ = element_tables()
    smooth_x, stiff_x, mass_x = line_operators(4)
    smooth_y, stiff_y, mass_y = line_operators(2)
    nodes = np.kron(np.kron(np.eye(4), to_nodes), np.kron(np.eye(2), to_nodes))

    def block(dx, dy):
        x, y = slice(16 * (dx + 1), 16 * (dx + 2)), slice(8 * (dy + 1), 8 * (dy + 2))
        return np.kron(smooth_x[:, x], smooth_y[:, y]) - 0.01 * (
            np.kron(stiff_x[:, x], mass_y[:, y]) + np.kron(mass_x[:, x], stiff_y[:, y])
        )

    cell_sums = np.zeros((32, 128))
    cell_sums[:] = np.kron(np.kron(np.eye(4), to_cells), np.kron(np.eye(2), to_cells))
    mine = block(0, 0)
    own = np.zeros((128, 128))
    own[:, :32] = mine @ nodes
    outer, inner = np.zeros((128, 128)), np.zeros((128, 128))
    halo = np.zeros((128, 128))
    pick = np.zeros((CELLS, 128), np.float32)
    pick[:32, :32] = np.eye(32)
    for slot, (dx, dy) in enumerate(SLOTS):
        part = block(dx, dy)
        left, scale, right = np.linalg.svd(part)
        rank = int((scale > 1e-10).sum())
        assert rank <= STATE_ROWS[slot]
        at = STATE_AT[slot]
        outer[:, at : at + rank] = left[:, :rank] * np.sqrt(scale[:rank])
        inner[at : at + rank] = right[:rank] * np.sqrt(scale[:rank])[:, None]
        cells = part @ nodes
        used = np.flatnonzero(np.abs(cells).max(axis=0) > 1e-12)
        assert len(used) <= CELL_ROWS[slot]
        at = CELL_AT[slot]
        halo[:, at : at + len(used)] = cells[:, used]
        pick[32 + at + np.arange(len(used)), used] = 1.0
    pieces = []
    for matrix in (cell_sums, inner, mine, outer, own, halo):
        pieces.extend(split(matrix))
    matrices = np.concatenate(pieces, axis=0)

    cell = np.arange(128)
    same = (cell[:, None] // 32) == (cell[None, :] // 32)
    step = (cell[:, None] - cell[None, :]) % 32
    east, west = same & (step == 1), same & (step == 31)
    along = np.concatenate([1.0 * east + 1.0 * west - same / 16.0, 1.0 * east - 1.0 * west], axis=1)
    along = np.concatenate([along, along], axis=0).astype(jnp.bfloat16)

    spread = np.zeros((128, 384))
    for s in range(2):
        for pair in range(2):
            for field in range(3):
                at = field * 128 + pair * 64 + s * 32
                spread[s * 8 + pair * 4 + field, at : at + 32] = 1.0
    means = (spread[:16] / 32.0).astype(jnp.bfloat16)
    spread = np.concatenate([spread, spread], axis=0).astype(jnp.bfloat16)
    return matrices, along, spread, means, pick


def halves(value):
    high = value.astype(BF16)
    return high, (value - high.astype(F32)).astype(BF16)


def dot(left, right):
    return jnp.dot(left, right, preferred_element_type=F32)


def dot_split(left, right):
    high, low = halves(right)
    return dot(left[0], high) + dot(left[1], high) + dot(left[0], low)


def iota(shape, axis):
    return lax.broadcasted_iota(jnp.int32, shape, axis)


def levels_moved(field, row):
    up = jnp.where(row == CRM_LEV - 1, field, pltpu.roll(field, 63, 0))
    down = jnp.where(row == 0, field, pltpu.roll(field, 1, 0))
    return up + down


def transported(field, along, momentum, row):
    return (
        0.4 * field
        + 0.15 * (along[:, :128] + levels_moved(field, row))
        + momentum * along[:, 128:]
    )


def condensed(heat, water, wet, saturation):
    cond = wet * jnp.maximum(water - 0.5 * heat - saturation, 0.0)
    return heat + 0.8 * cond, water - cond


def kernel(
    dyn, crm, mask, span, matrices, along_in, spread_in, means_in, pick_in,
    dyn_out, crm_out,
    xin, xb, mk, sp, mat, along, spread, means, pick,
    spans, xs, ys, wt, cat, og, ar, rs, rt, dh, dr, hs, hr, ob, od, place,
    load_sem, store_sem, go_sem, come_sem,
):
    p, r = lax.axis_index("blk"), lax.axis_index("row")
    rows, blocks = lax.axis_size("row"), lax.axis_size("blk")
    loads = [
        pltpu.make_async_copy(source, target, load_sem.at[k])
        for k, (source, target) in enumerate(
            ((span, sp), (dyn, xin), (matrices, mat), (pick_in, pick), (along_in, along),
             (crm, xb), (mask, mk), (spread_in, spread), (means_in, means))
        )
    ]
    for load in loads:
        load.start()

    barrier = pltpu.get_barrier_semaphore()

    def greet(k, carry):
        pl.semaphore_signal(
            barrier, inc=1, device_id=(p, lax.rem(r + k, rows)), device_id_type=MESH
        )
        return carry

    lax.fori_loop(1, rows, greet, None)
    around = [
        (lax.rem(p + blocks - dx, blocks), lax.rem(r + rows - dy, rows)) for dx, dy in SLOTS
    ]
    for slot in range(2, 8):
        pl.semaphore_signal(barrier, inc=1, device_id=around[slot], device_id_type=MESH)

    xs[...] = jnp.zeros_like(xs)
    wt[...] = jnp.zeros_like(wt)
    cat[...] = jnp.zeros_like(cat)
    spans[...] = jnp.zeros_like(spans)
    hr[HALO:128, :] = jnp.zeros((128 - HALO, 384), F32)

    def table(k, lines=128):
        at = (0, 64, 320, 576, 832, 1088)[k]
        return mat[at : at + lines], mat[at + lines : at + 2 * lines]

    loads[0].wait()
    spans[0:1, 0:32] = sp[...].astype(F32)
    named = spans[...]
    named = named + pltpu.roll(named, 32, 1)
    named = named + pltpu.roll(named, 64, 1)
    lane, line = iota((32, 128), 1), iota((32, 128), 0)
    across = jnp.broadcast_to(named[0:1, :], (32, 128))
    down = jnp.sum(jnp.where(lane == line, across, 0.0), axis=1, keepdims=True)
    earlier = jnp.where((down == across) & (line < (lane & 31)), 1.0, 0.0)
    position = 2.0 * named[0:1, :] + jnp.sum(earlier, axis=0, keepdims=True)
    lane, line = iota((128, 128), 1), iota((128, 128), 0)
    wanted = (2 * line - (line & 3)).astype(F32)
    offered = 4.0 * jnp.broadcast_to(position, (128, 128)) + (lane >> 5).astype(F32)
    send_to = jnp.concatenate(
        [jnp.where(offered - 4.0 * s == wanted, 1.0, 0.0) for s in range(2)], axis=1
    ).astype(BF16)

    loads[1].wait()
    loads[2].wait()
    for field in range(3):
        cat[32 * field : 32 * field + 32, 0:LEV] = dot_split(table(0, 32), xin[field])
    first = jnp.where(lane < CRM_LEV, cat[...], 0.0)
    high, low = halves(jnp.concatenate([first, pltpu.roll(first, 64, 1)], axis=0))
    sent = dot(send_to, jnp.concatenate([high, low], axis=1))
    og[...] = (sent[:, :128] + sent[:, 128:]).reshape(32, 4, 128)

    pl.semaphore_wait(barrier, rows - 1 + 6)

    def profile_copy(target):
        return pltpu.make_async_remote_copy(
            src_ref=og.at[target], dst_ref=ar.at[r], send_sem=go_sem.at[0],
            recv_sem=come_sem.at[0], device_id=(p, target), device_id_type=MESH,
        )

    def send_profile(k, carry):
        away = 16 + (1 - 2 * (k & 1)) * ((k + 1) >> 1)
        profile_copy(lax.rem(r + away, rows)).start()
        return carry

    lax.fori_loop(0, rows - 1, send_profile, None)
    ar[r] = og[r]

    for field in range(4):
        dh[:, 128 * field : 128 * field + LEV] = dot_split(table(1), xin[field])
    state_copies = []
    for slot in range(8):
        at = pl.ds(STATE_AT[slot], STATE_ROWS[slot])
        state_copies.append(
            pltpu.make_async_remote_copy(
                src_ref=dh.at[at], dst_ref=dr.at[at], send_sem=go_sem.at[1],
                recv_sem=come_sem.at[1], device_id=around[slot], device_id_type=MESH,
            )
        )
        state_copies[-1].start()

    for k in range(4, 9):
        loads[k].wait()
    row = iota((64, 128), 0)
    saturation = 0.5 - row.astype(F32) / CRM_LEV

    def begin(j, carry):
        at = pl.ds(pl.multiple_of(j * 128, 128), 128)
        for field in range(3):
            xs[j, 64 * field : 64 * field + CRM_LEV, :] = xb[field, :, at].astype(F32)
        wt[j, 0:CRM_LEV, :] = 0.5 * mk[:, at].astype(F32)
        state = xs[j]
        shifted = dot(state.astype(BF16), along[0:128, :])
        momentum = -0.1 * state[128:192]
        for field in range(3):
            part = slice(64 * field, 64 * field + 64)
            ys[j, part, :] = transported(state[part], shifted[part], momentum, row)
        return carry

    lax.fori_loop(0, 16, begin, None, unroll=2)

    for field in range(4):
        od[field] = dot_split(table(2), xin[field])

    loads[3].wait()
    back = jnp.sum(pick[...] * jnp.broadcast_to(position, (CELLS, 128)), axis=1, keepdims=True)
    lane = iota((CELLS, 128), 1)
    code = (2 * lane - (lane & 3)).astype(F32)
    for field in range(3):
        place[field] = jnp.concatenate(
            [jnp.where(4.0 * back + field - 4.0 * s == code, 1.0, 0.0) for s in range(2)], axis=1
        ).astype(BF16)

    def all_of(source, target, k):
        return pltpu.make_async_remote_copy(
            src_ref=source.at[pl.ds(0, 31)], dst_ref=target.at[pl.ds(0, 31)],
            send_sem=go_sem.at[k], recv_sem=come_sem.at[k],
            device_id=(p, lax.rem(r + 1, rows)), device_id_type=MESH,
        )

    all_of(og, ar, 0).wait_recv()
    forcing = ar[...].reshape(128, 128).T

    def tendency_copy(target):
        return pltpu.make_async_remote_copy(
            src_ref=rs.at[target], dst_ref=rt.at[r], send_sem=go_sem.at[2],
            recv_sem=come_sem.at[2], device_id=(p, target), device_id_type=MESH,
        )

    def finish(k, carry):
        away = 8 + (1 - 2 * (k & 1)) * ((k + 1) >> 1)
        j = lax.rem((r >> 1) + away, 16)
        at = pl.ds(pl.multiple_of(j * 128, 128), 128)
        shift = lax.rem(128 - 8 * j, 128)
        lane = iota((64, 128), 1)
        near = jnp.where(
            lane < 8,
            pltpu.roll(forcing[0:64], shift, 1),
            pltpu.roll(forcing[64:128], lax.rem(shift + 8, 128), 1),
        )
        near = jnp.where(lane < 16, near, 0.0)
        pulled = 0.3 * dot(jnp.concatenate(halves(near), axis=1), spread[...])
        wet = wt[j]
        one = [
            ys[j, 64 * field : 64 * field + 64, :] + pulled[:, 128 * field : 128 * field + 128]
            for field in range(3)
        ]
        one[0], one[1] = condensed(one[0], one[1], wet, saturation)
        both = [jnp.concatenate(halves(value), axis=1) for value in one]
        shifted = dot(jnp.concatenate(both, axis=0), along[...])
        momentum = -0.1 * one[2]
        two = [
            transported(one[field], shifted[64 * field : 64 * field + 64], momentum, row)
            + pulled[:, 128 * field : 128 * field + 128]
            for field in range(3)
        ]
        two[0], two[1] = condensed(two[0], two[1], wet, saturation)
        change = []
        for field in range(3):
            ob[field, :, at] = two[field][0:CRM_LEV].astype(BF16)
            change.append(halves(two[field] - xs[j, 64 * field : 64 * field + 64, :]))
        change = jnp.concatenate(
            [jnp.concatenate([c[half] for c in change], axis=1) for half in range(2)], axis=0
        )
        mean = lax.dot_general(
            means[...], change, (((1,), (1,)), ((), ())), preferred_element_type=F32
        )
        mean = mean + pltpu.roll(mean, 64, 1)
        message = jnp.where(iota((8, 128), 1) < 64, mean[0:8], mean[8:16])
        for pair in range(2):
            target = 2 * j + pair
            rs[target] = message[4 * pair : 4 * pair + 4]

            @pl.when(target != r)
            def _():
                tendency_copy(target).start()

        return carry

    lax.fori_loop(0, 16, finish, None, unroll=2)
    rt[r] = rs[r]

    store = pltpu.make_async_copy(ob, crm_out, store_sem.at[0])
    store.start()

    pltpu.make_async_remote_copy(
        src_ref=dh, dst_ref=dr, send_sem=go_sem.at[1], recv_sem=come_sem.at[1],
        device_id=around[0], device_id_type=MESH,
    ).wait_recv()
    for field in range(4):
        od[field] += dot_split(table(3), dr[:, 128 * field : 128 * field + 128])[:, 0:LEV]

    all_of(rs, rt, 2).wait_recv()
    given = rt[...].reshape(128, 128)
    lane = iota((128, 128), 1)
    given = jnp.concatenate(
        [jnp.where(lane < CRM_LEV, value, 0.0) for value in (given, pltpu.roll(given, 64, 1))],
        axis=0,
    )
    given = jnp.concatenate(halves(given), axis=1)
    cells = []
    for field in range(3):
        taken = dot(place[field], given)
        cells.append(taken[:, :128] + taken[:, 128:])
        hs[:, 128 * field : 128 * field + 128] = cells[field][32:]
    cell_copies = []
    for slot in range(8):
        at = pl.ds(CELL_AT[slot], CELL_ROWS[slot])
        cell_copies.append(
            pltpu.make_async_remote_copy(
                src_ref=hs.at[at], dst_ref=hr.at[at], send_sem=go_sem.at[3],
                recv_sem=come_sem.at[3], device_id=around[slot], device_id_type=MESH,
            )
        )
        cell_copies[-1].start()
    own = table(4)
    own = own[0][:, 0:32], own[1][:, 0:32]
    for field in range(3):
        od[field] += dot_split(own, cells[field][0:32])[:, 0:LEV]

    halo_copy = pltpu.make_async_remote_copy(
        src_ref=hs, dst_ref=hr.at[pl.ds(0, HALO)], send_sem=go_sem.at[3],
        recv_sem=come_sem.at[3], device_id=around[0], device_id_type=MESH,
    )
    halo_copy.wait_recv()
    for field in range(3):
        od[field] += dot_split(table(5), hr[:, 128 * field : 128 * field + 128])[:, 0:LEV]
    final = pltpu.make_async_copy(od, dyn_out, store_sem.at[1])
    final.start()
    all_of(og, ar, 0).wait_send()
    all_of(rs, rt, 2).wait_send()
    pltpu.make_async_remote_copy(
        src_ref=dh, dst_ref=dr, send_sem=go_sem.at[1], recv_sem=come_sem.at[1],
        device_id=around[0], device_id_type=MESH,
    ).wait_send()
    halo_copy.wait_send()
    store.wait()
    final.wait()


def per_device(dyn_state, crm_state, cloud_mask, span_of):
    consts = tuple(jnp.asarray(value) for value in tables())
    vmem = pltpu.VMEM
    scratch = [
        vmem((4, 128, LEV), F32), vmem((3, CRM_LEV, 2048), BF16), vmem((CRM_LEV, 2048), jnp.int32),
        vmem((1, 32), jnp.int32),
    ]
    scratch += [vmem(value.shape, value.dtype) for value in consts]
    scratch += [
        vmem((8, 128), F32),
        vmem((16, 192, 128), F32), vmem((16, 192, 128), F32), vmem((16, 64, 128), F32),
        vmem((128, 128), F32),
        vmem((32, 4, 128), F32), vmem((32, 4, 128), F32),
        vmem((32, 4, 128), F32), vmem((32, 4, 128), F32),
        vmem((128, 512), F32), vmem((128, 512), F32),
        vmem((HALO, 384), F32), vmem((128, 384), F32),
        vmem((3, CRM_LEV, 2048), BF16), vmem((4, 128, LEV), F32),
        vmem((3, CELLS, 256), BF16),
        pltpu.SemaphoreType.DMA((9,)), pltpu.SemaphoreType.DMA((2,)),
        pltpu.SemaphoreType.DMA((4,)), pltpu.SemaphoreType.DMA((4,)),
    ]
    nodes = dyn_state.transpose(0, 2, 3, 1).reshape(4, 128, LEV)
    dyn, crm = pl.pallas_call(
        kernel,
        out_shape=(
            jax.ShapeDtypeStruct((4, 128, LEV), F32),
            jax.ShapeDtypeStruct((3, CRM_LEV, 2048), BF16),
        ),
        in_specs=[pl.BlockSpec(memory_space=pl.ANY)] * 9,
        out_specs=[pl.BlockSpec(memory_space=pl.ANY)] * 2,
        scratch_shapes=scratch,
        compiler_params=pltpu.CompilerParams(
            collective_id=0, has_side_effects=True, vmem_limit_bytes=40 * 2**20
        ),
        name="physics_step",
    )(nodes, crm_state, cloud_mask, span_of.T, *consts)
    return dyn.reshape(4, 16, 8, LEV).transpose(0, 3, 1, 2), crm


def solution(mesh):
    return jax.shard_map(
        per_device,
        mesh=mesh,
        in_specs=(
            P(None, None, "blk", "row"),
            P(None, None, ("blk", "row")),
            P(None, ("blk", "row")),
            P(("blk", "row"), None),
        ),
        out_specs=(P(None, None, "blk", "row"), P(None, None, ("blk", "row"))),
        check_vma=False,
    )
```

time: 154 us -> 47.5 us (0.31)
  other arithmetic: 46.2 us -> 0 us
  local copies, waits for them, and re-layouts: 51 us -> 9.75 us
  Pallas kernels: 0 us -> 36.7 us
  starting transfers between devices: 36.5 us -> 0 us
  waiting for transfers between devices: 13.4 us -> 0 us
  matrix products: 4.59 us -> 0 us
    pallas_call x0 -> x1, Pallas kernels: none -> 36.7 us  [per_device(): pl.pallas_call(kernel, out_shape=(jax.ShapeDtypeStruct((4, 128, LEV), F32...]
    slice x29 -> x0, local copies, waits for them, and re-layouts: 23.6 us -> none  [the longest x10 13.1 us: transport(): upper = jnp.concatenate([field[1:], field[-1:]], axis=0)]
    all_to_all x2 -> x0, starting transfers between devices: 21.2 us -> none  [the longest x1 12 us: per_device(): lax.all_to_all(outgoing, 'row', split_axis=2, concat_axis=2, tiled=True)]
    reduce_sum x10 -> x0, other arithmetic: 19.2 us -> none  [the longest x9 18.4 us: slot_mean(): return field.reshape(field.shape[0], -1, ncols).mean(axis=2)]
    another operation x6 -> x0, other arithmetic: 18.5 us -> none  [the longest x3 11.4 us: cloud_model(): final = jnp.stack(fields).astype(jnp.bfloat16)]
    ppermute x8 -> x0, starting transfers between devices: 15.3 us -> none  [the longest x4 9.93 us: with_halo(): lax.ppermute(lax.slice_in_dim(block, 0, width, axis=dim), axis, backward)]
    concatenate x10 -> x0, local copies, waits for them, and re-layouts: 13.6 us -> none  [the longest x4 5.09 us: transport(): jnp.roll(field, -1, axis=1)]
    all_to_all x2 -> x0, waiting for transfers between devices: 8.79 us -> none  [the longest x1 8.79 us: per_device(): lax.all_to_all(tendency, 'row', split_axis=2, concat_axis=2, tiled=True)]
  transfers between devices with their start and end apart: 10 -> 0, of which waited for: 4 -> 0; matrix products, arithmetic and copies ran while one was open for 28% -> 0% of each run, Pallas kernels for 0% -> 0%
where the time goes in v1:
time: 47.5 us; the launch traced here: 47.1 us
  Pallas kernels  36.7 us (77%)
  local copies, waits for them, and re-layouts  9.75 us (21%)
  between operations  0.66 us (1%)
    pallas_call x1, Pallas kernels, per_device(): pl.pallas_call(kernel, out_shape=(jax.ShapeDtypeStruct((4, 128, LEV), F32...  36.7 us
    unnamed x20, local copies, waits for them, and re-layouts  9.75 us

profile of v1, /device:TPU:1, one launch (start us, length us, event | category | flops | bytes accessed | tf_op | source)
XLA Modules:
  0.0 47.1 jit_solution(3297171655363462397)
XLA Ops:
  0.6 0.0 copy-start.8
  0.6 0.6 %copy-done.8 = s32[32,1]{0,1:T(1,128)S(1)} copy-done((s32[32,1]{0,1:T(1,128)S(1)}, s32[32,1]{0,1:T(1,128)}, u32[]{:S(2)}) %copy-start.8) | copy-done | bytes 152
  1.3 0.0 copy-start
  1.3 1.1 %copy-done = bf16[3,58,2048]{2,1,0:T(8,128)(2,1)S(1)} copy-done((bf16[3,58,2048]{2,1,0:T(8,128)(2,1)S(1)}, bf16[3,58,2048]{2,1,0:T(8,128)(2,1)}, u32[]{:S(2)}) %copy-start) | copy-done | bytes 712728
  2.4 0.0 copy-start.1
  2.4 1.0 %copy-done.1 = s32[58,2048]{1,0:T(8,128)S(1)} copy-done((s32[58,2048]{1,0:T(8,128)S(1)}, s32[58,2048]{1,0:T(8,128)}, u32[]{:S(2)}) %copy-start.1) | copy-done | bytes 475160
  3.5 0.0 copy-start.2
  3.5 1.0 %copy-done.2 = bf16[1344,128]{1,0:T(8,128)(2,1)S(1)} copy-done((bf16[1344,128]{1,0:T(8,128)(2,1)S(1)}, bf16[1344,128]{1,0:T(8,128)(2,1)}, u32[]{:S(2)}) %copy-start.2) | copy-done | bytes 344088
  4.4 0.0 copy-start.3
  4.4 0.9 %copy-done.3 = f32[4,72,16,8]{1,3,2,0:T(8,128)S(1)} copy-done((f32[4,72,16,8]{1,3,2,0:T(8,128)S(1)}, f32[4,72,16,8]{1,3,2,0:T(8,128)}, u32[]{:S(2)}) %copy-start.3) | copy-done | bytes 147480
  5.4 0.0 copy-start.4
  5.4 0.9 %copy-done.4 = bf16[256,384]{1,0:T(8,128)(2,1)S(1)} copy-done((bf16[256,384]{1,0:T(8,128)(2,1)S(1)}, bf16[256,384]{1,0:T(8,128)(2,1)}, u32[]{:S(2)}) %copy-start.4) | copy-done | bytes 196632
  6.3 0.0 copy-start.5
  6.3 0.9 %copy-done.5 = bf16[256,256]{1,0:T(8,128)(2,1)S(1)} copy-done((bf16[256,256]{1,0:T(8,128)(2,1)S(1)}, bf16[256,256]{1,0:T(8,128)(2,1)}, u32[]{:S(2)}) %copy-start.5) | copy-done | bytes 131096
  7.2 0.0 copy-start.6
  7.2 0.9 %copy-done.6 = f32[144,128]{1,0:T(8,128)S(1)} copy-done((f32[144,128]{1,0:T(8,128)S(1)}, f32[144,128]{1,0:T(8,128)}, u32[]{:S(2)}) %copy-start.6) | copy-done | bytes 73752
  8.1 0.0 copy-start.7
  8.1 0.7 %copy-done.7 = bf16[16,384]{1,0:T(8,128)(2,1)S(1)} copy-done((bf16[16,384]{1,0:T(8,128)(2,1)S(1)}, bf16[16,384]{1,0:T(8,128)(2,1)}, u32[]{:S(2)}) %copy-start.7) | copy-done | bytes 12312
  8.8 36.7 %physics_step.1 = (f32[4,128,72]{2,1,0:T(8,128)S(1)}, bf16[3,58,2048]{2,1,0:T(8,128)(2,1)S(1)}) custom-call(f32[4,128,72]{2,1,0:T(8,128)S(1)} %bitcast.7, bf16[3,58,2048]{2,1,0:T(8,128)(2,1)S(1)} %copy-done, s32[58,2048]{1,0:T(8,128)S(1)} %copy-done.1, s32[1,32]{1,0:T(1,128)S(1)} %bitcast.9, bf16[1344,128]{1,0:T(8,128)(2,1)S(1)} %copy-done.2, ...), custom_call_target="tpu_custom_call" | custom-call | tf_op jit(solution)/shard_map/physics_step/pallas_call | solution.py:461
  45.6 0.7 %copy.13 = f32[4,72,16,8]{1,3,2,0:T(8,128)} copy(f32[4,72,16,8]{1,3,2,0:T(8,128)S(1)} %bitcast.8) | data formatting | bytes 294912
  46.3 0.9 %copy.14 = bf16[3,58,2048]{2,1,0:T(8,128)(2,1)} copy(bf16[3,58,2048]{2,1,0:T(8,128)(2,1)S(1)} %get-tuple-element.9) | data formatting | bytes 1425408
Async XLA Ops:
  0.6 0.7 %copy-start.8 = (s32[32,1]{0,1:T(1,128)S(1)}, s32[32,1]{0,1:T(1,128)}, u32[]{:S(2)}) copy-start(s32[32,1]{0,1:T(1,128)} %param.12) | copy-start | bytes 388
  1.3 1.1 %copy-start = (bf16[3,58,2048]{2,1,0:T(8,128)(2,1)S(1)}, bf16[3,58,2048]{2,1,0:T(8,128)(2,1)}, u32[]{:S(2)}) copy-start(bf16[3,58,2048]{2,1,0:T(8,128)(2,1)} %crm.1) | copy-start | bytes 2138116
  2.4 1.0 %copy-start.1 = (s32[58,2048]{1,0:T(8,128)S(1)}, s32[58,2048]{1,0:T(8,128)}, u32[]{:S(2)}) copy-start(s32[58,2048]{1,0:T(8,128)} %mask.1) | copy-start | bytes 1425412
  3.5 1.0 %copy-start.2 = (bf16[1344,128]{1,0:T(8,128)(2,1)S(1)}, bf16[1344,128]{1,0:T(8,128)(2,1)}, u32[]{:S(2)}) copy-start(bf16[1344,128]{1,0:T(8,128)(2,1)} %constant.10.clone.matrices) | copy-start | bytes 1032196
  4.4 0.9 %copy-start.3 = (f32[4,72,16,8]{1,3,2,0:T(8,128)S(1)}, f32[4,72,16,8]{1,3,2,0:T(8,128)}, u32[]{:S(2)}) copy-start(f32[4,72,16,8]{1,3,2,0:T(8,128)} %param.9) | copy-start | bytes 442372
  5.4 0.9 %copy-start.4 = (bf16[256,384]{1,0:T(8,128)(2,1)S(1)}, bf16[256,384]{1,0:T(8,128)(2,1)}, u32[]{:S(2)}) copy-start(bf16[256,384]{1,0:T(8,128)(2,1)} %constant.12.clone.spread_in) | copy-start | bytes 589828
  6.3 0.9 %copy-start.5 = (bf16[256,256]{1,0:T(8,128)(2,1)S(1)}, bf16[256,256]{1,0:T(8,128)(2,1)}, u32[]{:S(2)}) copy-start(bf16[256,256]{1,0:T(8,128)(2,1)} %constant.11.clone.along_in) | copy-start | bytes 393220
  7.2 0.9 %copy-start.6 = (f32[144,128]{1,0:T(8,128)S(1)}, f32[144,128]{1,0:T(8,128)}, u32[]{:S(2)}) copy-start(f32[144,128]{1,0:T(8,128)} %constant.14.clone.pick_in) | copy-start | bytes 221188
  8.1 0.7 %copy-start.7 = (bf16[16,384]{1,0:T(8,128)(2,1)S(1)}, bf16[16,384]{1,0:T(8,128)(2,1)}, u32[]{:S(2)}) copy-start(bf16[16,384]{1,0:T(8,128)(2,1)} %constant.13.clone.means_in) | copy-start | bytes 36868

commit v2 on v1

--- a/solution.py
+++ b/solution.py
@@ -13,11 +13,12 @@
 F32, BF16 = jnp.float32, jnp.bfloat16
 SLOTS = ((0, -1), (0, 1), (-1, 0), (1, 0), (-1, -1), (-1, 1), (1, -1), (1, 1))
 STATE_ROWS = (32, 32, 16, 16, 8, 8, 8, 8)
+TILES, GROUPS = 4, 4
+CELL_RANK = (16, 16, 8, 8, 2, 2, 2, 2)
 CELL_ROWS = (24, 24, 16, 16, 8, 8, 8, 8)
 STATE_AT = tuple(int(v) for v in np.cumsum((0,) + STATE_ROWS))
 CELL_AT = tuple(int(v) for v in np.cumsum((0,) + CELL_ROWS))
 HALO = CELL_AT[-1]
-CELLS = 32 + HALO
 
 
 def poly_times(first_poly, second_poly):
@@ -101,9 +102,9 @@
     own = np.zeros((128, 128))
     own[:, :32] = mine @ nodes
     outer, inner = np.zeros((128, 128)), np.zeros((128, 128))
-    halo = np.zeros((128, 128))
-    pick = np.zeros((CELLS, 128), np.float32)
-    pick[:32, :32] = np.eye(32)
+    arrive = np.zeros((3, 128, 256))
+    leave = np.zeros((2, HALO, 128))
+    pick = np.zeros((HALO, 256), np.float32)
     for slot, (dx, dy) in enumerate(SLOTS):
         part = block(dx, dy)
         left, scale, right = np.linalg.svd(part)
@@ -112,16 +113,22 @@
         at = STATE_AT[slot]
         outer[:, at : at + rank] = left[:, :rank] * np.sqrt(scale[:rank])
         inner[at : at + rank] = right[:rank] * np.sqrt(scale[:rank])[:, None]
-        cells = part @ nodes
-        used = np.flatnonzero(np.abs(cells).max(axis=0) > 1e-12)
-        assert len(used) <= CELL_ROWS[slot]
-        at = CELL_AT[slot]
-        halo[:, at : at + len(used)] = cells[:, used]
-        pick[32 + at + np.arange(len(used)), used] = 1.0
+        left, scale, right = np.linalg.svd(part @ nodes, full_matrices=False)
+        rank = int((scale > 1e-10).sum())
+        assert rank <= CELL_RANK[slot]
+        left, right = left * np.sqrt(scale), right * np.sqrt(scale)[:, None]
+        half = CELL_RANK[slot] // 2
+        for field in range(3):
+            at = CELL_AT[slot] + field * half
+            pick[at : at + half, field::4] = 1.0
+            for h in range(2):
+                leave[h, at : at + half, :32] = right[h : 2 * half : 2]
+                arrive[field, :, h * HALO + at : h * HALO + at + half] = left[:, h : 2 * half : 2]
     pieces = []
-    for matrix in (cell_sums, inner, mine, outer, own, halo):
+    for matrix in (cell_sums, inner, mine, outer, own, leave[0], leave[1]):
         pieces.extend(split(matrix))
     matrices = np.concatenate(pieces, axis=0)
+    arrive = np.concatenate(split(arrive.reshape(384, 256)), axis=0)
 
     cell = np.arange(128)
     same = (cell[:, None] // 32) == (cell[None, :] // 32)
@@ -130,15 +137,18 @@
     along = np.concatenate([1.0 * east + 1.0 * west - same / 16.0, 1.0 * east - 1.0 * west], axis=1)
     along = np.concatenate([along, along], axis=0).astype(jnp.bfloat16)
 
-    spread = np.zeros((128, 384))
+    spread = np.zeros((16, 384))
     for s in range(2):
         for pair in range(2):
             for field in range(3):
                 at = field * 128 + pair * 64 + s * 32
                 spread[s * 8 + pair * 4 + field, at : at + 32] = 1.0
-    means = (spread[:16] / 32.0).astype(jnp.bfloat16)
-    spread = np.concatenate([spread, spread], axis=0).astype(jnp.bfloat16)
-    return matrices, along, spread, means, pick
+    means = (spread / 32.0).astype(jnp.bfloat16)
+    wide = np.zeros((2, 2, TILES, 8, TILES, 384))
+    for tile in range(TILES):
+        wide[:, :, tile, :, tile] = spread.reshape(1, 2, 8, 384)
+    spread = wide.reshape(32 * TILES, 384 * TILES).astype(jnp.bfloat16)
+    return matrices, along, spread, means, pick, arrive
 
 
 def halves(value):
@@ -179,19 +189,19 @@
 
 
 def kernel(
-    dyn, crm, mask, span, matrices, along_in, spread_in, means_in, pick_in,
+    dyn, crm, mask, span, matrices, along_in, spread_in, means_in, pick_in, arrive_in,
     dyn_out, crm_out,
-    xin, xb, mk, sp, mat, along, spread, means, pick,
-    spans, xs, ys, wt, cat, og, ar, rs, rt, dh, dr, hs, hr, ob, od, place,
-    load_sem, store_sem, go_sem, come_sem,
+    xin, xb, mk, sp, mat, along, spread, means, pick, arrive,
+    spans, xs, ys, wt, cat, og, ar, rs, rt, dh, dr, hs, hr, ob, od, place, post,
+    load_sem, store_sem, go_sem, come_sem, tile_sem,
 ):
     p, r = lax.axis_index("blk"), lax.axis_index("row")
     rows, blocks = lax.axis_size("row"), lax.axis_size("blk")
     loads = [
         pltpu.make_async_copy(source, target, load_sem.at[k])
         for k, (source, target) in enumerate(
-            ((span, sp), (dyn, xin), (matrices, mat), (pick_in, pick), (along_in, along),
-             (crm, xb), (mask, mk), (spread_in, spread), (means_in, means))
+            ((span, sp), (dyn, xin), (matrices, mat), (crm, xb), (mask, mk), (along_in, along),
+             (spread_in, spread), (means_in, means), (pick_in, pick), (arrive_in, arrive))
         )
     ]
     for load in loads:
@@ -212,14 +222,11 @@
     for slot in range(2, 8):
         pl.semaphore_signal(barrier, inc=1, device_id=around[slot], device_id_type=MESH)
 
-    xs[...] = jnp.zeros_like(xs)
-    wt[...] = jnp.zeros_like(wt)
     cat[...] = jnp.zeros_like(cat)
     spans[...] = jnp.zeros_like(spans)
-    hr[HALO:128, :] = jnp.zeros((128 - HALO, 384), F32)
 
     def table(k, lines=128):
-        at = (0, 64, 320, 576, 832, 1088)[k]
+        at = (0, 64, 320, 576, 832, 1088, 1088 + 2 * HALO)[k]
         return mat[at : at + lines], mat[at + lines : at + 2 * lines]
 
     loads[0].wait()
@@ -253,7 +260,7 @@
     def profile_copy(target):
         return pltpu.make_async_remote_copy(
             src_ref=og.at[target], dst_ref=ar.at[r], send_sem=go_sem.at[0],
-            recv_sem=come_sem.at[0], device_id=(p, target), device_id_type=MESH,
+            recv_sem=tile_sem.at[lax.div(r, 2 * TILES)], device_id=(p, target), device_id_type=MESH,
         )
 
     def send_profile(k, carry):
@@ -263,6 +270,14 @@
 
     lax.fori_loop(0, rows - 1, send_profile, None)
     ar[r] = og[r]
+
+    def clear(j, carry):
+        for field in range(3):
+            xs[j, 64 * field + 56 : 64 * field + 64, :] = jnp.zeros((8, 128), F32)
+        wt[j, 56:64, :] = jnp.zeros((8, 128), F32)
+        return carry
+
+    lax.fori_loop(0, 16, clear, None, unroll=4)
 
     for field in range(4):
         dh[:, 128 * field : 128 * field + LEV] = dot_split(table(1), xin[field])
@@ -277,7 +292,7 @@
         )
         state_copies[-1].start()
 
-    for k in range(4, 9):
+    for k in range(3, 6):
         loads[k].wait()
     row = iota((64, 128), 0)
     saturation = 0.5 - row.astype(F32) / CRM_LEV
@@ -300,14 +315,25 @@
     for field in range(4):
         od[field] = dot_split(table(2), xin[field])
 
-    loads[3].wait()
-    back = jnp.sum(pick[...] * jnp.broadcast_to(position, (CELLS, 128)), axis=1, keepdims=True)
-    lane = iota((CELLS, 128), 1)
-    code = (2 * lane - (lane & 3)).astype(F32)
+    for k in range(6, 10):
+        loads[k].wait()
+    lane, line = iota((32, 128), 1), iota((32, 128), 0)
+    home = jnp.sum(
+        jnp.where(lane == line, jnp.broadcast_to(position, (32, 128)), 0.0), axis=1, keepdims=True
+    )
+    code = (lane >> 2).astype(F32)
+    match = jnp.concatenate(
+        [jnp.where(home - s == 2.0 * code, 1.0, 0.0) for s in range(2)], axis=1
+    )
+    lane = iota((32, 256), 1)
     for field in range(3):
-        place[field] = jnp.concatenate(
-            [jnp.where(4.0 * back + field - 4.0 * s == code, 1.0, 0.0) for s in range(2)], axis=1
-        ).astype(BF16)
+        place[32 * field : 32 * field + 32, :] = jnp.where((lane & 3) == field, match, 0.0).astype(BF16)
+    match = match.astype(BF16)
+    for h in range(2):
+        for half, piece in enumerate(table(5 + h, HALO)):
+            post[half * HALO : (half + 1) * HALO, 256 * h : 256 * h + 256] = (
+                pick[...] * dot(piece[:, 0:32], match)
+            ).astype(BF16)
 
     def all_of(source, target, k):
         return pltpu.make_async_remote_copy(
@@ -316,66 +342,75 @@
             device_id=(p, lax.rem(r + 1, rows)), device_id_type=MESH,
         )
 
-    all_of(og, ar, 0).wait_recv()
-    forcing = ar[...].reshape(128, 128).T
-
     def tendency_copy(target):
         return pltpu.make_async_remote_copy(
             src_ref=rs.at[target], dst_ref=rt.at[r], send_sem=go_sem.at[2],
             recv_sem=come_sem.at[2], device_id=(p, target), device_id_type=MESH,
         )
 
-    def finish(k, carry):
-        away = 8 + (1 - 2 * (k & 1)) * ((k + 1) >> 1)
-        j = lax.rem((r >> 1) + away, 16)
-        at = pl.ds(pl.multiple_of(j * 128, 128), 128)
-        shift = lax.rem(128 - 8 * j, 128)
-        lane = iota((64, 128), 1)
-        near = jnp.where(
-            lane < 8,
-            pltpu.roll(forcing[0:64], shift, 1),
-            pltpu.roll(forcing[64:128], lax.rem(shift + 8, 128), 1),
-        )
-        near = jnp.where(lane < 16, near, 0.0)
-        pulled = 0.3 * dot(jnp.concatenate(halves(near), axis=1), spread[...])
-        wet = wt[j]
-        one = [
-            ys[j, 64 * field : 64 * field + 64, :] + pulled[:, 128 * field : 128 * field + 128]
-            for field in range(3)
+    mine = lax.div(r, 2 * TILES)
+
+    def finish(group, own):
+        first = pl.multiple_of(group * TILES, TILES)
+        near = ar.at[pl.ds(2 * first, 2 * TILES)]
+        due = ar.at[pl.ds(2 * first, 2 * TILES - own)]
+        pltpu.make_async_copy(due, due, tile_sem.at[group]).wait()
+        near = near[...].reshape(8 * TILES, 128)
+        near = jnp.concatenate([near, pltpu.roll(near, 64, 1)], axis=0)
+        high, low = halves(near)
+        near = jnp.concatenate([high.astype(F32), low.astype(F32)], axis=0).T[0:64]
+        pulled = 0.3 * dot(near.astype(BF16), spread[...])
+        pulled = [
+            [pulled[:, 128 * (3 * t + f) : 128 * (3 * t + f + 1)] for f in range(3)]
+            for t in range(TILES)
         ]
-        one[0], one[1] = condensed(one[0], one[1], wet, saturation)
-        both = [jnp.concatenate(halves(value), axis=1) for value in one]
+        fields = []
+        for t in range(TILES):
+            one = [ys[first + t, 64 * f : 64 * f + 64, :] + pulled[t][f] for f in range(3)]
+            one[0], one[1] = condensed(one[0], one[1], wt[first + t], saturation)
+            fields.append(one)
+        both = [jnp.concatenate(halves(value), axis=1) for one in fields for value in one]
         shifted = dot(jnp.concatenate(both, axis=0), along[...])
-        momentum = -0.1 * one[2]
-        two = [
-            transported(one[field], shifted[64 * field : 64 * field + 64], momentum, row)
-            + pulled[:, 128 * field : 128 * field + 128]
-            for field in range(3)
-        ]
-        two[0], two[1] = condensed(two[0], two[1], wet, saturation)
         change = []
-        for field in range(3):
-            ob[field, :, at] = two[field][0:CRM_LEV].astype(BF16)
-            change.append(halves(two[field] - xs[j, 64 * field : 64 * field + 64, :]))
-        change = jnp.concatenate(
-            [jnp.concatenate([c[half] for c in change], axis=1) for half in range(2)], axis=0
-        )
+        for t in range(TILES):
+            at = pl.ds(pl.multiple_of(128 * (first + t), 128), 128)
+            one = fields[t]
+            momentum = -0.1 * one[2]
+            two = []
+            for f in range(3):
+                line = 64 * (3 * t + f)
+                moved = transported(one[f], shifted[line : line + 64], momentum, row)
+                two.append(moved + pulled[t][f])
+            two[0], two[1] = condensed(two[0], two[1], wt[first + t], saturation)
+            parts = []
+            for f in range(3):
+                ob[f, :, at] = two[f][0:CRM_LEV].astype(BF16)
+                parts.append(halves(two[f] - xs[first + t, 64 * f : 64 * f + 64, :]))
+            change += [jnp.concatenate([part[h] for part in parts], axis=1) for h in range(2)]
         mean = lax.dot_general(
-            means[...], change, (((1,), (1,)), ((), ())), preferred_element_type=F32
-        )
-        mean = mean + pltpu.roll(mean, 64, 1)
-        message = jnp.where(iota((8, 128), 1) < 64, mean[0:8], mean[8:16])
-        for pair in range(2):
-            target = 2 * j + pair
-            rs[target] = message[4 * pair : 4 * pair + 4]
-
-            @pl.when(target != r)
-            def _():
+            means[...], jnp.concatenate(change, axis=0), (((1,), (1,)), ((), ())),
+            preferred_element_type=F32,
+        )
+        for t in range(TILES):
+            part = mean[:, 128 * t : 128 * t + 128]
+            part = part + pltpu.roll(part, 64, 1)
+            message = jnp.where(iota((8, 128), 1) < 64, part[0:8], part[8:16])
+            for pair in range(2):
+                rs[2 * (first + t) + pair] = message[4 * pair : 4 * pair + 4]
+        for k in range(2 * TILES):
+            target = 2 * first + k
+            if own:
+                pl.when(target != r)(tendency_copy(target).start)
+            else:
                 tendency_copy(target).start()
 
+    def others(k, carry):
+        away = GROUPS // 2 + (1 - 2 * (k & 1)) * ((k + 1) >> 1)
+        finish(lax.rem(mine + away, GROUPS), 0)
         return carry
 
-    lax.fori_loop(0, 16, finish, None, unroll=2)
+    lax.fori_loop(0, GROUPS - 1, others, None)
+    finish(mine, 1)
     rt[r] = rs[r]
 
     store = pltpu.make_async_copy(ob, crm_out, store_sem.at[0])
@@ -391,16 +426,13 @@
     all_of(rs, rt, 2).wait_recv()
     given = rt[...].reshape(128, 128)
     lane = iota((128, 128), 1)
-    given = jnp.concatenate(
-        [jnp.where(lane < CRM_LEV, value, 0.0) for value in (given, pltpu.roll(given, 64, 1))],
-        axis=0,
-    )
-    given = jnp.concatenate(halves(given), axis=1)
-    cells = []
-    for field in range(3):
-        taken = dot(place[field], given)
-        cells.append(taken[:, :128] + taken[:, 128:])
-        hs[:, 128 * field : 128 * field + 128] = cells[field][32:]
+    given = [jnp.where(lane < CRM_LEV, value, 0.0) for value in (given, pltpu.roll(given, 64, 1))]
+    given = jnp.concatenate(halves(jnp.concatenate(given, axis=0)), axis=1)
+    turned = jnp.concatenate(
+        [pltpu.roll(given[:, 128 * k : 128 * k + 128].astype(F32), 64, 1) for k in range(2)], axis=1
+    ).astype(BF16)
+    sent = dot(post[...], jnp.concatenate([given, turned], axis=0))
+    hs[...] = sent[0:HALO, 0:128] + sent[0:HALO, 128:256] + sent[HALO:, 0:128]
     cell_copies = []
     for slot in range(8):
         at = pl.ds(CELL_AT[slot], CELL_ROWS[slot])
@@ -411,18 +443,27 @@
             )
         )
         cell_copies[-1].start()
+    cells = dot(place[...], given)
+    cells = cells[:, 0:128] + cells[:, 128:256]
     own = table(4)
     own = own[0][:, 0:32], own[1][:, 0:32]
     for field in range(3):
-        od[field] += dot_split(own, cells[field][0:32])[:, 0:LEV]
+        od[field] += dot_split(own, cells[32 * field : 32 * field + 32])[:, 0:LEV]
 
     halo_copy = pltpu.make_async_remote_copy(
-        src_ref=hs, dst_ref=hr.at[pl.ds(0, HALO)], send_sem=go_sem.at[3],
+        src_ref=hs, dst_ref=hr, send_sem=go_sem.at[3],
         recv_sem=come_sem.at[3], device_id=around[0], device_id_type=MESH,
     )
     halo_copy.wait_recv()
+    lane = iota((HALO, 128), 1)
+    came = hr[...]
+    came = [jnp.where(lane < 64, value, 0.0) for value in (came, pltpu.roll(came, 64, 1))]
+    came = jnp.concatenate(came + [jnp.zeros((256 - 2 * HALO, 128), F32)], axis=0)
+    came = jnp.concatenate(halves(came), axis=1)
     for field in range(3):
-        od[field] += dot_split(table(5), hr[:, 128 * field : 128 * field + 128])[:, 0:LEV]
+        high = dot(arrive[128 * field : 128 * field + 128, :], came)
+        low = dot(arrive[384 + 128 * field : 512 + 128 * field, :], came[:, 0:128])
+        od[field] += (high[:, 0:128] + high[:, 128:256] + low)[:, 0:LEV]
     final = pltpu.make_async_copy(od, dyn_out, store_sem.at[1])
     final.start()
     all_of(og, ar, 0).wait_send()
@@ -451,27 +492,28 @@
         vmem((32, 4, 128), F32), vmem((32, 4, 128), F32),
         vmem((32, 4, 128), F32), vmem((32, 4, 128), F32),
         vmem((128, 512), F32), vmem((128, 512), F32),
-        vmem((HALO, 384), F32), vmem((128, 384), F32),
+        vmem((HALO, 128), F32), vmem((HALO, 128), F32),
         vmem((3, CRM_LEV, 2048), BF16), vmem((4, 128, LEV), F32),
-        vmem((3, CELLS, 256), BF16),
-        pltpu.SemaphoreType.DMA((9,)), pltpu.SemaphoreType.DMA((2,)),
-        pltpu.SemaphoreType.DMA((4,)), pltpu.SemaphoreType.DMA((4,)),
+        vmem((96, 256), BF16), vmem((2 * HALO, 512), BF16),
+        pltpu.SemaphoreType.DMA((10,)), pltpu.SemaphoreType.DMA((2,)),
+        pltpu.SemaphoreType.DMA((4,)), pltpu.SemaphoreType.DMA((4,)), pltpu.SemaphoreType.DMA((GROUPS,)),
     ]
     nodes = dyn_state.transpose(0, 2, 3, 1).reshape(4, 128, LEV)
+    operands = (nodes, crm_state, cloud_mask, span_of.T, *consts)
     dyn, crm = pl.pallas_call(
         kernel,
         out_shape=(
             jax.ShapeDtypeStruct((4, 128, LEV), F32),
             jax.ShapeDtypeStruct((3, CRM_LEV, 2048), BF16),
         ),
-        in_specs=[pl.BlockSpec(memory_space=pl.ANY)] * 9,
+        in_specs=[pl.BlockSpec(memory_space=pl.ANY)] * 10,
         out_specs=[pl.BlockSpec(memory_space=pl.ANY)] * 2,
         scratch_shapes=scratch,
         compiler_params=pltpu.CompilerParams(
             collective_id=0, has_side_effects=True, vmem_limit_bytes=40 * 2**20
         ),
         name="physics_step",
-    )(nodes, crm_state, cloud_mask, span_of.T, *consts)
+    )(*(pltpu.with_memory_space_constraint(value, pltpu.HBM) for value in operands))
     return dyn.reshape(4, 16, 8, LEV).transpose(0, 3, 1, 2), crm
 
 

time: 47.5 us -> 32.5 us (0.68)
  local copies, waits for them, and re-layouts: 9.75 us -> 1.58 us
  Pallas kernels: 36.7 us -> 30.2 us
    unnamed x20 -> x2, local copies, waits for them, and re-layouts: 9.75 us -> 1.58 us
    pallas_call x1, Pallas kernels: 36.7 us -> 30.2 us  [per_device(): pl.pallas_call(kernel, out_shape=(jax.ShapeDtypeStruct((4, 128, LEV), F32...]
where the time goes in v2:
time: 32.5 us; the launch traced here: 32.4 us
  Pallas kernels  30.2 us (93%)
  local copies, waits for them, and re-layouts  1.58 us (5%)
  between operations  0.64 us (2%)
    pallas_call x1, Pallas kernels, per_device(): pl.pallas_call(kernel, out_shape=(jax.ShapeDtypeStruct((4, 128, LEV), F32...  30.2 us
    unnamed x2, local copies, waits for them, and re-layouts  1.58 us

profile of v2, /device:TPU:1, one launch (start us, length us, event | category | flops | bytes accessed | tf_op | source)
XLA Modules:
  0.0 32.4 jit_solution(5170818112763749250)
XLA Ops:
  0.6 30.2 %physics_step.1 = (f32[4,128,72]{2,1,0:T(8,128)S(1)}, bf16[3,58,2048]{2,1,0:T(8,128)(2,1)S(1)}) custom-call(f32[4,128,72]{2,1,0:T(8,128)} %bitcast.8, bf16[3,58,2048]{2,1,0:T(8,128)(2,1)} %crm.1, s32[58,2048]{1,0:T(8,128)} %mask.1, s32[1,32]{1,0:T(1,128)} %bitcast.9, bf16[1536,128]{1,0:T(8,128)(2,1)} %constant.12.clone.matrices, ...), custom_call_target="tpu_custom_call" | custom-call | tf_op jit(solution)/shard_map/physics_step/pallas_call | solution.py:503
  30.8 0.7 %copy.14 = f32[4,72,16,8]{1,3,2,0:T(8,128)} copy(f32[4,72,16,8]{1,3,2,0:T(8,128)S(1)} %bitcast.7) | data formatting | bytes 294912
  31.5 0.9 %copy.15 = bf16[3,58,2048]{2,1,0:T(8,128)(2,1)} copy(bf16[3,58,2048]{2,1,0:T(8,128)(2,1)S(1)} %get-tuple-element.9) | data formatting | bytes 1425408

commit v3 on v2

--- a/solution.py
+++ b/solution.py
@@ -125,9 +125,10 @@
                 leave[h, at : at + half, :32] = right[h : 2 * half : 2]
                 arrive[field, :, h * HALO + at : h * HALO + at + half] = left[:, h : 2 * half : 2]
     pieces = []
-    for matrix in (cell_sums, inner, mine, outer, own, leave[0], leave[1]):
+    for matrix in (inner, mine, outer, own, leave[0], leave[1]):
         pieces.extend(split(matrix))
     matrices = np.concatenate(pieces, axis=0)
+    cell_sums = np.concatenate(split(cell_sums), axis=0)
     arrive = np.concatenate(split(arrive.reshape(384, 256)), axis=0)
 
     cell = np.arange(128)
@@ -148,7 +149,7 @@
     for tile in range(TILES):
         wide[:, :, tile, :, tile] = spread.reshape(1, 2, 8, 384)
     spread = wide.reshape(32 * TILES, 384 * TILES).astype(jnp.bfloat16)
-    return matrices, along, spread, means, pick, arrive
+    return cell_sums, matrices, along, spread, means, pick, arrive
 
 
 def halves(value):
@@ -189,44 +190,45 @@
 
 
 def kernel(
-    dyn, crm, mask, span, matrices, along_in, spread_in, means_in, pick_in, arrive_in,
-    dyn_out, crm_out,
-    xin, xb, mk, sp, mat, along, spread, means, pick, arrive,
-    spans, xs, ys, wt, cat, og, ar, rs, rt, dh, dr, hs, hr, ob, od, place, post,
+    dyn, crm, mask, span, sums_in, matrices, along_in, spread_in, means_in, pick_in,
+    hr, part_out, crm_out,
+    xin, xb, mk, sp, sums, mat, along, spread, means, pick,
+    spans, xs, ys, wt, cat, og, ar, rs, rt, dh, dr, hs, ob, od, place, post,
     load_sem, store_sem, go_sem, come_sem, tile_sem,
 ):
     p, r = lax.axis_index("blk"), lax.axis_index("row")
     rows, blocks = lax.axis_size("row"), lax.axis_size("blk")
-    loads = [
-        pltpu.make_async_copy(source, target, load_sem.at[k])
-        for k, (source, target) in enumerate(
-            ((span, sp), (dyn, xin), (matrices, mat), (crm, xb), (mask, mk), (along_in, along),
-             (spread_in, spread), (means_in, means), (pick_in, pick), (arrive_in, arrive))
-        )
-    ]
-    for load in loads:
-        load.start()
-
     barrier = pltpu.get_barrier_semaphore()
 
+    def far_first(k):
+        return lax.rem(r + 16 + (1 - 2 * (k & 1)) * ((k + 1) >> 1), rows)
+
     def greet(k, carry):
-        pl.semaphore_signal(
-            barrier, inc=1, device_id=(p, lax.rem(r + k, rows)), device_id_type=MESH
-        )
+        pl.semaphore_signal(barrier, inc=1, device_id=(p, far_first(k)), device_id_type=MESH)
         return carry
 
-    lax.fori_loop(1, rows, greet, None)
+    lax.fori_loop(0, rows - 1, greet, None)
     around = [
         (lax.rem(p + blocks - dx, blocks), lax.rem(r + rows - dy, rows)) for dx, dy in SLOTS
     ]
     for slot in range(2, 8):
         pl.semaphore_signal(barrier, inc=1, device_id=around[slot], device_id_type=MESH)
 
+    loads = [
+        pltpu.make_async_copy(source, target, load_sem.at[k])
+        for k, (source, target) in enumerate(
+            ((span, sp), (sums_in, sums), (dyn, xin), (crm, xb), (mask, mk), (along_in, along),
+             (spread_in, spread), (means_in, means), (matrices, mat), (pick_in, pick))
+        )
+    ]
+    for load in loads[:3]:
+        load.start()
+
     cat[...] = jnp.zeros_like(cat)
     spans[...] = jnp.zeros_like(spans)
 
     def table(k, lines=128):
-        at = (0, 64, 320, 576, 832, 1088, 1088 + 2 * HALO)[k]
+        at = (0, 256, 512, 768, 1024, 1024 + 2 * HALO)[k]
         return mat[at : at + lines], mat[at + lines : at + 2 * lines]
 
     loads[0].wait()
@@ -248,8 +250,10 @@
 
     loads[1].wait()
     loads[2].wait()
+    for load in loads[3:6]:
+        load.start()
     for field in range(3):
-        cat[32 * field : 32 * field + 32, 0:LEV] = dot_split(table(0, 32), xin[field])
+        cat[32 * field : 32 * field + 32, 0:LEV] = dot_split((sums[0:32], sums[32:64]), xin[field])
     first = jnp.where(lane < CRM_LEV, cat[...], 0.0)
     high, low = halves(jnp.concatenate([first, pltpu.roll(first, 64, 1)], axis=0))
     sent = dot(send_to, jnp.concatenate([high, low], axis=1))
@@ -264,76 +268,43 @@
         )
 
     def send_profile(k, carry):
-        away = 16 + (1 - 2 * (k & 1)) * ((k + 1) >> 1)
-        profile_copy(lax.rem(r + away, rows)).start()
+        away = (1 - 2 * (k & 1)) * ((k + 2) >> 1)
+        profile_copy(lax.rem(r + rows + away, rows)).start()
         return carry
 
     lax.fori_loop(0, rows - 1, send_profile, None)
     ar[r] = og[r]
 
-    def clear(j, carry):
-        for field in range(3):
-            xs[j, 64 * field + 56 : 64 * field + 64, :] = jnp.zeros((8, 128), F32)
-        wt[j, 56:64, :] = jnp.zeros((8, 128), F32)
-        return carry
-
-    lax.fori_loop(0, 16, clear, None, unroll=4)
-
-    for field in range(4):
-        dh[:, 128 * field : 128 * field + LEV] = dot_split(table(1), xin[field])
-    state_copies = []
-    for slot in range(8):
-        at = pl.ds(STATE_AT[slot], STATE_ROWS[slot])
-        state_copies.append(
-            pltpu.make_async_remote_copy(
-                src_ref=dh.at[at], dst_ref=dr.at[at], send_sem=go_sem.at[1],
-                recv_sem=come_sem.at[1], device_id=around[slot], device_id_type=MESH,
-            )
-        )
-        state_copies[-1].start()
+    for load in loads[6:]:
+        load.start()
 
     for k in range(3, 6):
         loads[k].wait()
     row = iota((64, 128), 0)
     saturation = 0.5 - row.astype(F32) / CRM_LEV
-
-    def begin(j, carry):
-        at = pl.ds(pl.multiple_of(j * 128, 128), 128)
-        for field in range(3):
-            xs[j, 64 * field : 64 * field + CRM_LEV, :] = xb[field, :, at].astype(F32)
-        wt[j, 0:CRM_LEV, :] = 0.5 * mk[:, at].astype(F32)
-        state = xs[j]
-        shifted = dot(state.astype(BF16), along[0:128, :])
-        momentum = -0.1 * state[128:192]
-        for field in range(3):
-            part = slice(64 * field, 64 * field + 64)
-            ys[j, part, :] = transported(state[part], shifted[part], momentum, row)
+    rest = jnp.zeros((64 - CRM_LEV, 128), F32)
+
+    def begin(group, carry):
+        first = pl.multiple_of(group * TILES, TILES)
+        state = []
+        for t in range(TILES):
+            at = pl.ds(pl.multiple_of(128 * (first + t), 128), 128)
+            wt[first + t] = jnp.concatenate([0.5 * mk[:, at].astype(F32), rest], axis=0)
+            for f in range(3):
+                state.append(jnp.concatenate([xb[f, :, at].astype(F32), rest], axis=0))
+                xs[first + t, 64 * f : 64 * f + 64, :] = state[-1]
+        shifted = dot(jnp.concatenate(state, axis=0).astype(BF16), along[0:128, :])
+        for t in range(TILES):
+            momentum = -0.1 * state[3 * t + 2]
+            for f in range(3):
+                line = 64 * (3 * t + f)
+                moved = transported(state[3 * t + f], shifted[line : line + 64], momentum, row)
+                ys[first + t, 64 * f : 64 * f + 64, :] = moved
         return carry
 
-    lax.fori_loop(0, 16, begin, None, unroll=2)
-
-    for field in range(4):
-        od[field] = dot_split(table(2), xin[field])
-
-    for k in range(6, 10):
-        loads[k].wait()
-    lane, line = iota((32, 128), 1), iota((32, 128), 0)
-    home = jnp.sum(
-        jnp.where(lane == line, jnp.broadcast_to(position, (32, 128)), 0.0), axis=1, keepdims=True
-    )
-    code = (lane >> 2).astype(F32)
-    match = jnp.concatenate(
-        [jnp.where(home - s == 2.0 * code, 1.0, 0.0) for s in range(2)], axis=1
-    )
-    lane = iota((32, 256), 1)
-    for field in range(3):
-        place[32 * field : 32 * field + 32, :] = jnp.where((lane & 3) == field, match, 0.0).astype(BF16)
-    match = match.astype(BF16)
-    for h in range(2):
-        for half, piece in enumerate(table(5 + h, HALO)):
-            post[half * HALO : (half + 1) * HALO, 256 * h : 256 * h + 256] = (
-                pick[...] * dot(piece[:, 0:32], match)
-            ).astype(BF16)
+    lax.fori_loop(0, GROUPS, begin, None)
+    loads[6].wait()
+    loads[7].wait()
 
     def all_of(source, target, k):
         return pltpu.make_async_remote_copy(
@@ -405,23 +376,52 @@
                 tendency_copy(target).start()
 
     def others(k, carry):
-        away = GROUPS // 2 + (1 - 2 * (k & 1)) * ((k + 1) >> 1)
-        finish(lax.rem(mine + away, GROUPS), 0)
+        away = (1 - 2 * (k & 1)) * ((k + 2) >> 1)
+        finish(lax.rem(mine + GROUPS + away, GROUPS), 0)
         return carry
 
+    finish(mine, 1)
     lax.fori_loop(0, GROUPS - 1, others, None)
-    finish(mine, 1)
     rt[r] = rs[r]
 
     store = pltpu.make_async_copy(ob, crm_out, store_sem.at[0])
     store.start()
 
-    pltpu.make_async_remote_copy(
-        src_ref=dh, dst_ref=dr, send_sem=go_sem.at[1], recv_sem=come_sem.at[1],
-        device_id=around[0], device_id_type=MESH,
-    ).wait_recv()
+    loads[8].wait()
     for field in range(4):
-        od[field] += dot_split(table(3), dr[:, 128 * field : 128 * field + 128])[:, 0:LEV]
+        dh[:, 128 * field : 128 * field + LEV] = dot_split(table(0), xin[field])
+    state_copies = []
+    for slot in range(8):
+        at = pl.ds(STATE_AT[slot], STATE_ROWS[slot])
+        state_copies.append(
+            pltpu.make_async_remote_copy(
+                src_ref=dh.at[at], dst_ref=dr.at[at], send_sem=go_sem.at[1],
+                recv_sem=come_sem.at[1], device_id=around[slot], device_id_type=MESH,
+            )
+        )
+        state_copies[-1].start()
+
+    loads[9].wait()
+    lane, line = iota((32, 128), 1), iota((32, 128), 0)
+    home = jnp.sum(
+        jnp.where(lane == line, jnp.broadcast_to(position, (32, 128)), 0.0), axis=1, keepdims=True
+    )
+    code = (lane >> 2).astype(F32)
+    match = jnp.concatenate(
+        [jnp.where(home - s == 2.0 * code, 1.0, 0.0) for s in range(2)], axis=1
+    )
+    lane = iota((32, 256), 1)
+    for field in range(3):
+        place[32 * field : 32 * field + 32, :] = jnp.where((lane & 3) == field, match, 0.0).astype(BF16)
+    match = match.astype(BF16)
+    for h in range(2):
+        for half, piece in enumerate(table(4 + h, HALO)):
+            post[half * HALO : (half + 1) * HALO, 256 * h : 256 * h + 256] = (
+                pick[...] * dot(piece[:, 0:32], match)
+            ).astype(BF16)
+
+    for field in range(4):
+        od[field, :, 0:LEV] = dot_split(table(1), xin[field])
 
     all_of(rs, rt, 2).wait_recv()
     given = rt[...].reshape(128, 128)
@@ -445,27 +445,25 @@
         cell_copies[-1].start()
     cells = dot(place[...], given)
     cells = cells[:, 0:128] + cells[:, 128:256]
-    own = table(4)
+    own = table(3)
     own = own[0][:, 0:32], own[1][:, 0:32]
     for field in range(3):
-        od[field] += dot_split(own, cells[32 * field : 32 * field + 32])[:, 0:LEV]
+        od[field, :, 0:LEV] += dot_split(own, cells[32 * field : 32 * field + 32])[:, 0:LEV]
+
+    pltpu.make_async_remote_copy(
+        src_ref=dh, dst_ref=dr, send_sem=go_sem.at[1], recv_sem=come_sem.at[1],
+        device_id=around[0], device_id_type=MESH,
+    ).wait_recv()
+    for field in range(4):
+        od[field, :, 0:LEV] += dot_split(table(2), dr[:, 128 * field : 128 * field + 128])[:, 0:LEV]
 
     halo_copy = pltpu.make_async_remote_copy(
         src_ref=hs, dst_ref=hr, send_sem=go_sem.at[3],
         recv_sem=come_sem.at[3], device_id=around[0], device_id_type=MESH,
     )
+    part = pltpu.make_async_copy(od, part_out, store_sem.at[1])
+    part.start()
     halo_copy.wait_recv()
-    lane = iota((HALO, 128), 1)
-    came = hr[...]
-    came = [jnp.where(lane < 64, value, 0.0) for value in (came, pltpu.roll(came, 64, 1))]
-    came = jnp.concatenate(came + [jnp.zeros((256 - 2 * HALO, 128), F32)], axis=0)
-    came = jnp.concatenate(halves(came), axis=1)
-    for field in range(3):
-        high = dot(arrive[128 * field : 128 * field + 128, :], came)
-        low = dot(arrive[384 + 128 * field : 512 + 128 * field, :], came[:, 0:128])
-        od[field] += (high[:, 0:128] + high[:, 128:256] + low)[:, 0:LEV]
-    final = pltpu.make_async_copy(od, dyn_out, store_sem.at[1])
-    final.start()
     all_of(og, ar, 0).wait_send()
     all_of(rs, rt, 2).wait_send()
     pltpu.make_async_remote_copy(
@@ -474,11 +472,35 @@
     ).wait_send()
     halo_copy.wait_send()
     store.wait()
-    final.wait()
+    part.wait()
+
+
+def last_kernel(came_in, part, arrive_in, crm_in, dyn_out, crm_out, arrive, od, sem):
+    crm = pltpu.make_async_copy(crm_in, crm_out, sem.at[0])
+    load = pltpu.make_async_copy(arrive_in, arrive, sem.at[1])
+    load.start()
+    crm.start()
+    stores = [pltpu.make_async_copy(od.at[f], dyn_out.at[f], sem.at[2 + f]) for f in range(4)]
+    od[3] = part[3, :, 0:LEV]
+    stores[3].start()
+    lane = iota((HALO, 128), 1)
+    came = came_in[...]
+    came = [jnp.where(lane < 64, value, 0.0) for value in (came, pltpu.roll(came, 64, 1))]
+    came = jnp.concatenate(came + [jnp.zeros((256 - 2 * HALO, 128), F32)], axis=0)
+    came = jnp.concatenate(halves(came), axis=1)
+    load.wait()
+    taken = dot(arrive[...], came)
+    for f in range(3):
+        high, low = taken[128 * f : 128 * f + 128], taken[384 + 128 * f : 512 + 128 * f]
+        od[f] = part[f, :, 0:LEV] + (high[:, 0:128] + high[:, 128:256] + low[:, 0:128])[:, 0:LEV]
+        stores[f].start()
+    crm.wait()
+    for store in stores:
+        store.wait()
 
 
 def per_device(dyn_state, crm_state, cloud_mask, span_of):
-    consts = tuple(jnp.asarray(value) for value in tables())
+    *consts, arrive = (jnp.asarray(value) for value in tables())
     vmem = pltpu.VMEM
     scratch = [
         vmem((4, 128, LEV), F32), vmem((3, CRM_LEV, 2048), BF16), vmem((CRM_LEV, 2048), jnp.int32),
@@ -492,28 +514,42 @@
         vmem((32, 4, 128), F32), vmem((32, 4, 128), F32),
         vmem((32, 4, 128), F32), vmem((32, 4, 128), F32),
         vmem((128, 512), F32), vmem((128, 512), F32),
-        vmem((HALO, 128), F32), vmem((HALO, 128), F32),
-        vmem((3, CRM_LEV, 2048), BF16), vmem((4, 128, LEV), F32),
+        vmem((HALO, 128), F32),
+        vmem((3, CRM_LEV, 2048), BF16), vmem((4, 128, 128), F32),
         vmem((96, 256), BF16), vmem((2 * HALO, 512), BF16),
         pltpu.SemaphoreType.DMA((10,)), pltpu.SemaphoreType.DMA((2,)),
         pltpu.SemaphoreType.DMA((4,)), pltpu.SemaphoreType.DMA((4,)), pltpu.SemaphoreType.DMA((GROUPS,)),
     ]
     nodes = dyn_state.transpose(0, 2, 3, 1).reshape(4, 128, LEV)
     operands = (nodes, crm_state, cloud_mask, span_of.T, *consts)
-    dyn, crm = pl.pallas_call(
+    anywhere = pl.BlockSpec(memory_space=pl.ANY)
+    came, part, crm = pl.pallas_call(
         kernel,
         out_shape=(
-            jax.ShapeDtypeStruct((4, 128, LEV), F32),
-            jax.ShapeDtypeStruct((3, CRM_LEV, 2048), BF16),
+            vmem((HALO, 128), F32), vmem((4, 128, 128), F32), vmem((3, CRM_LEV, 2048), BF16)
         ),
-        in_specs=[pl.BlockSpec(memory_space=pl.ANY)] * 10,
-        out_specs=[pl.BlockSpec(memory_space=pl.ANY)] * 2,
+        in_specs=[anywhere] * 10,
+        out_specs=[anywhere] * 3,
         scratch_shapes=scratch,
         compiler_params=pltpu.CompilerParams(
             collective_id=0, has_side_effects=True, vmem_limit_bytes=40 * 2**20
         ),
         name="physics_step",
     )(*(pltpu.with_memory_space_constraint(value, pltpu.HBM) for value in operands))
+    near = pl.BlockSpec(memory_space=pltpu.VMEM)
+    dyn, crm = pl.pallas_call(
+        last_kernel,
+        out_shape=(
+            pltpu.HBM((4, 128, LEV), F32), pltpu.HBM((3, CRM_LEV, 2048), BF16)
+        ),
+        in_specs=[near, near, anywhere, anywhere],
+        out_specs=[anywhere] * 2,
+        scratch_shapes=[
+            vmem((768, 256), BF16), vmem((4, 128, LEV), F32), pltpu.SemaphoreType.DMA((6,))
+        ],
+        compiler_params=pltpu.CompilerParams(vmem_limit_bytes=8 * 2**20),
+        name="last_step",
+    )(came, part, arrive, crm)
     return dyn.reshape(4, 16, 8, LEV).transpose(0, 3, 1, 2), crm
 
 

time: 32.5 us -> 31.6 us (0.972)
  local copies, waits for them, and re-layouts: 1.58 us -> 0.01 us
  Pallas kernels: 30.2 us -> 30.8 us
    unnamed x2, local copies, waits for them, and re-layouts: 1.58 us -> 0.01 us
    pallas_call x1 -> x2, Pallas kernels: 30.2 us -> 30.8 us  [the longest x1 29.5 us: per_device(): pl.pallas_call(kernel, out_shape=(vmem((HALO, 128), F32), vmem((4, 128, 1...]
where the time goes in v3:
time: 31.6 us; the launch traced here: 31.4 us
  Pallas kernels  30.8 us (97%)
  between operations  0.65 us (2%)
    pallas_call x1, Pallas kernels, per_device(): pl.pallas_call(kernel, out_shape=(vmem((HALO, 128), F32), vmem((4, 128, 1...  29.5 us
    pallas_call x1, Pallas kernels, per_device(): pl.pallas_call(last_kernel, out_shape=(pltpu.HBM((4, 128, LEV), F32), plt...  1.24 us

profile of v3, /device:TPU:1, one launch (start us, length us, event | category | flops | bytes accessed | tf_op | source)
XLA Modules:
  0.0 31.4 jit_solution(17885702345448126638)
XLA Ops:
  0.6 0.0 copy-start
  0.6 29.5 %physics_step.1 = (f32[112,128]{1,0:T(8,128)S(1)}, f32[4,128,128]{2,1,0:T(8,128)S(1)}, bf16[3,58,2048]{2,1,0:T(8,128)(2,1)S(1)}) custom-call(f32[4,128,72]{2,1,0:T(8,128)} %bitcast.7, bf16[3,58,2048]{2,1,0:T(8,128)(2,1)} %crm.1, s32[58,2048]{1,0:T(8,128)} %mask.1, s32[1,32]{1,0:T(1,128)} %bitcast.8, bf16[64,128]{1,0:T(8,128)(2,1)} %constant.14.clone.sums_in, ...), custom_call_target="tpu_custom_call" | custom-call | tf_op jit(solution)/shard_map/physics_step/pallas_call | solution.py:526
  30.2 0.0 copy-done
  30.2 1.2 %last_step.1 = (f32[4,128,72]{2,1,0:T(8,128)}, bf16[3,58,2048]{2,1,0:T(8,128)(2,1)}) custom-call(f32[112,128]{1,0:T(8,128)S(1)} %get-tuple-element.7.came_in, f32[4,128,128]{2,1,0:T(8,128)S(1)} %get-tuple-element.8.part, bf16[768,256]{1,0:T(8,128)(2,1)S(1)} %copy-done, bf16[3,58,2048]{2,1,0:T(8,128)(2,1)S(1)} %get-tuple-element.9.crm_in), custom_call_target="tpu_custom_call" | custom-call | tf_op jit(solution)/shard_map/last_step/pallas_call | solution.py:540
Async XLA Ops:
  0.6 29.6 %copy-start = (bf16[768,256]{1,0:T(8,128)(2,1)S(1)}, bf16[768,256]{1,0:T(8,128)(2,1)}, u32[]{:S(2)}) copy-start(bf16[768,256]{1,0:T(8,128)(2,1)} %constant.20.clone.arrive_in) | copy-start | bytes 1179652

commit v4 on v3

--- a/solution.py
+++ b/solution.py
@@ -145,10 +145,7 @@
                 at = field * 128 + pair * 64 + s * 32
                 spread[s * 8 + pair * 4 + field, at : at + 32] = 1.0
     means = (spread / 32.0).astype(jnp.bfloat16)
-    wide = np.zeros((2, 2, TILES, 8, TILES, 384))
-    for tile in range(TILES):
-        wide[:, :, tile, :, tile] = spread.reshape(1, 2, 8, 384)
-    spread = wide.reshape(32 * TILES, 384 * TILES).astype(jnp.bfloat16)
+    spread = np.concatenate([spread, spread, np.zeros((96, 384))], axis=0).astype(jnp.bfloat16)
     return cell_sums, matrices, along, spread, means, pick, arrive
 
 
@@ -166,20 +163,33 @@
     return dot(left[0], high) + dot(left[1], high) + dot(left[0], low)
 
 
+def slot_means(weights, fields):
+    return lax.dot_general(
+        weights, fields, (((1,), (1,)), ((), ())), preferred_element_type=F32
+    )
+
+
 def iota(shape, axis):
     return lax.broadcasted_iota(jnp.int32, shape, axis)
 
 
-def levels_moved(field, row):
-    up = jnp.where(row == CRM_LEV - 1, field, pltpu.roll(field, 63, 0))
-    down = jnp.where(row == 0, field, pltpu.roll(field, 1, 0))
-    return up + down
-
-
-def transported(field, along, momentum, row):
+def levels_moved(field):
+    sub = iota((8, 128), 0)
+    rows = [field[8 * k : 8 * k + 8] for k in range(8)]
+    up = [pltpu.roll(value, 7, 0) for value in rows]
+    down = [pltpu.roll(value, 1, 0) for value in rows]
+    moved = []
+    for k in range(8):
+        above = jnp.where(sub == 7, up[k + 1], up[k]) if k < 7 else jnp.where(sub >= 1, rows[7], up[7])
+        below = jnp.where(sub == 0, down[k - 1] if k else rows[0], down[k])
+        moved.append(above + below)
+    return jnp.concatenate(moved, axis=0)
+
+
+def transported(field, along, momentum):
     return (
         0.4 * field
-        + 0.15 * (along[:, :128] + levels_moved(field, row))
+        + 0.15 * (along[:, :128] + levels_moved(field))
         + momentum * along[:, 128:]
     )
 
@@ -292,19 +302,25 @@
             wt[first + t] = jnp.concatenate([0.5 * mk[:, at].astype(F32), rest], axis=0)
             for f in range(3):
                 state.append(jnp.concatenate([xb[f, :, at].astype(F32), rest], axis=0))
-                xs[first + t, 64 * f : 64 * f + 64, :] = state[-1]
         shifted = dot(jnp.concatenate(state, axis=0).astype(BF16), along[0:128, :])
         for t in range(TILES):
             momentum = -0.1 * state[3 * t + 2]
             for f in range(3):
                 line = 64 * (3 * t + f)
-                moved = transported(state[3 * t + f], shifted[line : line + 64], momentum, row)
+                moved = transported(state[3 * t + f], shifted[line : line + 64], momentum)
                 ys[first + t, 64 * f : 64 * f + 64, :] = moved
+        start = jnp.concatenate(
+            [jnp.concatenate(state[3 * t : 3 * t + 3], axis=1) for t in range(TILES)], axis=0
+        )
+        mean = slot_means(means[...], start.astype(BF16))
+        for t in range(TILES):
+            part = mean[:, 64 * t : 64 * t + 64]
+            xs[first + t] = jnp.concatenate([part[0:8], part[8:16]], axis=1)
         return carry
 
+    loads[7].wait()
     lax.fori_loop(0, GROUPS, begin, None)
     loads[6].wait()
-    loads[7].wait()
 
     def all_of(source, target, k):
         return pltpu.make_async_remote_copy(
@@ -326,13 +342,15 @@
         near = ar.at[pl.ds(2 * first, 2 * TILES)]
         due = ar.at[pl.ds(2 * first, 2 * TILES - own)]
         pltpu.make_async_copy(due, due, tile_sem.at[group]).wait()
-        near = near[...].reshape(8 * TILES, 128)
-        near = jnp.concatenate([near, pltpu.roll(near, 64, 1)], axis=0)
-        high, low = halves(near)
-        near = jnp.concatenate([high.astype(F32), low.astype(F32)], axis=0).T[0:64]
-        pulled = 0.3 * dot(near.astype(BF16), spread[...])
+        near = 0.3 * near[...].reshape(8 * TILES, 128)
+        parts = [part.astype(F32) for part in (*halves(near), *halves(pltpu.roll(near, 64, 1)))]
+        near = jnp.concatenate(
+            [parts[k][8 * t : 8 * t + 8] for t in range(TILES) for k in (0, 2, 1, 3)], axis=0
+        ).T[0:64]
+        near = [near] + [pltpu.roll(near, 128 - 32 * t, 1) for t in range(1, TILES)]
+        pulled = dot(jnp.concatenate(near, axis=0).astype(BF16), spread[...])
         pulled = [
-            [pulled[:, 128 * (3 * t + f) : 128 * (3 * t + f + 1)] for f in range(3)]
+            [pulled[64 * t : 64 * t + 64, 128 * f : 128 * f + 128] for f in range(3)]
             for t in range(TILES)
         ]
         fields = []
@@ -350,22 +368,19 @@
             two = []
             for f in range(3):
                 line = 64 * (3 * t + f)
-                moved = transported(one[f], shifted[line : line + 64], momentum, row)
+                moved = transported(one[f], shifted[line : line + 64], momentum)
                 two.append(moved + pulled[t][f])
             two[0], two[1] = condensed(two[0], two[1], wt[first + t], saturation)
             parts = []
             for f in range(3):
-                ob[f, :, at] = two[f][0:CRM_LEV].astype(BF16)
-                parts.append(halves(two[f] - xs[first + t, 64 * f : 64 * f + 64, :]))
+                parts.append(halves(two[f]))
+                ob[f, :, at] = parts[f][0][0:CRM_LEV]
             change += [jnp.concatenate([part[h] for part in parts], axis=1) for h in range(2)]
-        mean = lax.dot_general(
-            means[...], jnp.concatenate(change, axis=0), (((1,), (1,)), ((), ())),
-            preferred_element_type=F32,
-        )
+        mean = slot_means(means[...], jnp.concatenate(change, axis=0))
         for t in range(TILES):
             part = mean[:, 128 * t : 128 * t + 128]
             part = part + pltpu.roll(part, 64, 1)
-            message = jnp.where(iota((8, 128), 1) < 64, part[0:8], part[8:16])
+            message = jnp.where(iota((8, 128), 1) < 64, part[0:8], part[8:16]) - xs[first + t]
             for pair in range(2):
                 rs[2 * (first + t) + pair] = message[4 * pair : 4 * pair + 4]
         for k in range(2 * TILES):
@@ -380,8 +395,8 @@
         finish(lax.rem(mine + GROUPS + away, GROUPS), 0)
         return carry
 
+    lax.fori_loop(0, GROUPS - 1, others, None)
     finish(mine, 1)
-    lax.fori_loop(0, GROUPS - 1, others, None)
     rt[r] = rs[r]
 
     store = pltpu.make_async_copy(ob, crm_out, store_sem.at[0])
@@ -416,7 +431,8 @@
     match = match.astype(BF16)
     for h in range(2):
         for half, piece in enumerate(table(4 + h, HALO)):
-            post[half * HALO : (half + 1) * HALO, 256 * h : 256 * h + 256] = (
+            at = (2 * half + h) * HALO
+            post[at : at + HALO, :] = (
                 pick[...] * dot(piece[:, 0:32], match)
             ).astype(BF16)
 
@@ -428,11 +444,10 @@
     lane = iota((128, 128), 1)
     given = [jnp.where(lane < CRM_LEV, value, 0.0) for value in (given, pltpu.roll(given, 64, 1))]
     given = jnp.concatenate(halves(jnp.concatenate(given, axis=0)), axis=1)
-    turned = jnp.concatenate(
-        [pltpu.roll(given[:, 128 * k : 128 * k + 128].astype(F32), 64, 1) for k in range(2)], axis=1
-    ).astype(BF16)
-    sent = dot(post[...], jnp.concatenate([given, turned], axis=0))
-    hs[...] = sent[0:HALO, 0:128] + sent[0:HALO, 128:256] + sent[HALO:, 0:128]
+    sent = dot(post[...], given)
+    sent = [sent[HALO * k : HALO * k + HALO] for k in range(4)]
+    sent = [sent[h][:, 0:128] + sent[h][:, 128:256] + sent[2 + h][:, 0:128] for h in range(2)]
+    hs[...] = sent[0] + pltpu.roll(sent[1], 64, 1)
     cell_copies = []
     for slot in range(8):
         at = pl.ds(CELL_AT[slot], CELL_ROWS[slot])
@@ -509,14 +524,14 @@
     scratch += [vmem(value.shape, value.dtype) for value in consts]
     scratch += [
         vmem((8, 128), F32),
-        vmem((16, 192, 128), F32), vmem((16, 192, 128), F32), vmem((16, 64, 128), F32),
+        vmem((16, 8, 128), F32), vmem((16, 192, 128), F32), vmem((16, 64, 128), F32),
         vmem((128, 128), F32),
         vmem((32, 4, 128), F32), vmem((32, 4, 128), F32),
         vmem((32, 4, 128), F32), vmem((32, 4, 128), F32),
         vmem((128, 512), F32), vmem((128, 512), F32),
         vmem((HALO, 128), F32),
         vmem((3, CRM_LEV, 2048), BF16), vmem((4, 128, 128), F32),
-        vmem((96, 256), BF16), vmem((2 * HALO, 512), BF16),
+        vmem((96, 256), BF16), vmem((4 * HALO, 256), BF16),
         pltpu.SemaphoreType.DMA((10,)), pltpu.SemaphoreType.DMA((2,)),
         pltpu.SemaphoreType.DMA((4,)), pltpu.SemaphoreType.DMA((4,)), pltpu.SemaphoreType.DMA((GROUPS,)),
     ]

time: 31.6 us -> 31.4 us (level)
  no operation moved by 1% of the time
where the time goes in v4:
time: 31.4 us; the launch traced here: 31.2 us
  Pallas kernels  30.6 us (97%)
  between operations  0.65 us (2%)
    pallas_call x1, Pallas kernels, per_device(): pl.pallas_call(kernel, out_shape=(vmem((HALO, 128), F32), vmem((4, 128, 1...  29.4 us
    pallas_call x1, Pallas kernels, per_device(): pl.pallas_call(last_kernel, out_shape=(pltpu.HBM((4, 128, LEV), F32), plt...  1.23 us

profile of v4, /device:TPU:1, one launch (start us, length us, event | category | flops | bytes accessed | tf_op | source)
XLA Modules:
  0.0 31.2 jit_solution(8124309229722528158)
XLA Ops:
  0.6 0.0 copy-start
  0.6 29.4 %physics_step.1 = (f32[112,128]{1,0:T(8,128)S(1)}, f32[4,128,128]{2,1,0:T(8,128)S(1)}, bf16[3,58,2048]{2,1,0:T(8,128)(2,1)S(1)}) custom-call(f32[4,128,72]{2,1,0:T(8,128)} %bitcast.7, bf16[3,58,2048]{2,1,0:T(8,128)(2,1)} %crm.1, s32[58,2048]{1,0:T(8,128)} %mask.1, s32[1,32]{1,0:T(1,128)} %bitcast.8, bf16[64,128]{1,0:T(8,128)(2,1)} %constant.14.clone.sums_in, ...), custom_call_target="tpu_custom_call" | custom-call | tf_op jit(solution)/shard_map/physics_step/pallas_call | solution.py:541
  30.0 0.0 copy-done
  30.0 1.2 %last_step.1 = (f32[4,128,72]{2,1,0:T(8,128)}, bf16[3,58,2048]{2,1,0:T(8,128)(2,1)}) custom-call(f32[112,128]{1,0:T(8,128)S(1)} %get-tuple-element.7.came_in, f32[4,128,128]{2,1,0:T(8,128)S(1)} %get-tuple-element.8.part, bf16[768,256]{1,0:T(8,128)(2,1)S(1)} %copy-done, bf16[3,58,2048]{2,1,0:T(8,128)(2,1)S(1)} %get-tuple-element.9.crm_in), custom_call_target="tpu_custom_call" | custom-call | tf_op jit(solution)/shard_map/last_step/pallas_call | solution.py:555
Async XLA Ops:
  0.6 29.4 %copy-start = (bf16[768,256]{1,0:T(8,128)(2,1)S(1)}, bf16[768,256]{1,0:T(8,128)(2,1)}, u32[]{:S(2)}) copy-start(bf16[768,256]{1,0:T(8,128)(2,1)} %constant.20.clone.arrive_in) | copy-start | bytes 1179652

commit v5 on v4

--- a/solution.py
+++ b/solution.py
@@ -217,7 +217,7 @@
         pl.semaphore_signal(barrier, inc=1, device_id=(p, far_first(k)), device_id_type=MESH)
         return carry
 
-    lax.fori_loop(0, rows - 1, greet, None)
+    lax.fori_loop(0, rows - 1, greet, None, unroll=True)
     around = [
         (lax.rem(p + blocks - dx, blocks), lax.rem(r + rows - dy, rows)) for dx, dy in SLOTS
     ]
@@ -278,11 +278,10 @@
         )
 
     def send_profile(k, carry):
-        away = (1 - 2 * (k & 1)) * ((k + 2) >> 1)
-        profile_copy(lax.rem(r + rows + away, rows)).start()
+        profile_copy(far_first(k)).start()
         return carry
 
-    lax.fori_loop(0, rows - 1, send_profile, None)
+    lax.fori_loop(0, rows - 1, send_profile, None, unroll=True)
     ar[r] = og[r]
 
     for load in loads[6:]:
@@ -448,16 +447,12 @@
     sent = [sent[HALO * k : HALO * k + HALO] for k in range(4)]
     sent = [sent[h][:, 0:128] + sent[h][:, 128:256] + sent[2 + h][:, 0:128] for h in range(2)]
     hs[...] = sent[0] + pltpu.roll(sent[1], 64, 1)
-    cell_copies = []
-    for slot in range(8):
+    for slot in (4, 5, 6, 7, 0, 1, 2, 3):
         at = pl.ds(CELL_AT[slot], CELL_ROWS[slot])
-        cell_copies.append(
-            pltpu.make_async_remote_copy(
-                src_ref=hs.at[at], dst_ref=hr.at[at], send_sem=go_sem.at[3],
-                recv_sem=come_sem.at[3], device_id=around[slot], device_id_type=MESH,
-            )
-        )
-        cell_copies[-1].start()
+        pltpu.make_async_remote_copy(
+            src_ref=hs.at[at], dst_ref=hr.at[at], send_sem=go_sem.at[3],
+            recv_sem=come_sem.at[3], device_id=around[slot], device_id_type=MESH,
+        ).start()
     cells = dot(place[...], given)
     cells = cells[:, 0:128] + cells[:, 128:256]
     own = table(3)
@@ -490,12 +485,10 @@
     part.wait()
 
 
-def last_kernel(came_in, part, arrive_in, crm_in, dyn_out, crm_out, arrive, od, sem):
+def last_kernel(came_in, part, arrive, crm_in, dyn_out, crm_out, od, sem):
     crm = pltpu.make_async_copy(crm_in, crm_out, sem.at[0])
-    load = pltpu.make_async_copy(arrive_in, arrive, sem.at[1])
-    load.start()
     crm.start()
-    stores = [pltpu.make_async_copy(od.at[f], dyn_out.at[f], sem.at[2 + f]) for f in range(4)]
+    stores = [pltpu.make_async_copy(od.at[f], dyn_out.at[f], sem.at[1 + f]) for f in range(4)]
     od[3] = part[3, :, 0:LEV]
     stores[3].start()
     lane = iota((HALO, 128), 1)
@@ -503,7 +496,6 @@
     came = [jnp.where(lane < 64, value, 0.0) for value in (came, pltpu.roll(came, 64, 1))]
     came = jnp.concatenate(came + [jnp.zeros((256 - 2 * HALO, 128), F32)], axis=0)
     came = jnp.concatenate(halves(came), axis=1)
-    load.wait()
     taken = dot(arrive[...], came)
     for f in range(3):
         high, low = taken[128 * f : 128 * f + 128], taken[384 + 128 * f : 512 + 128 * f]
@@ -557,10 +549,10 @@
         out_shape=(
             pltpu.HBM((4, 128, LEV), F32), pltpu.HBM((3, CRM_LEV, 2048), BF16)
         ),
-        in_specs=[near, near, anywhere, anywhere],
+        in_specs=[near, near, near, anywhere],
         out_specs=[anywhere] * 2,
         scratch_shapes=[
-            vmem((768, 256), BF16), vmem((4, 128, LEV), F32), pltpu.SemaphoreType.DMA((6,))
+            vmem((4, 128, LEV), F32), pltpu.SemaphoreType.DMA((5,))
         ],
         compiler_params=pltpu.CompilerParams(vmem_limit_bytes=8 * 2**20),
         name="last_step",

time: 31.4 us -> 30.8 us (0.981)
  Pallas kernels: 30.6 us -> 30 us
    pallas_call x1, Pallas kernels: 29.4 us -> 29 us  [per_device(): pl.pallas_call(kernel, out_shape=(vmem((HALO, 128), F32), vmem((4, 128, 1...]
where the time goes in v5:
time: 30.8 us; the launch traced here: 30.7 us
  Pallas kernels  30 us (97%)
  between operations  0.65 us (2%)
    pallas_call x1, Pallas kernels, per_device(): pl.pallas_call(kernel, out_shape=(vmem((HALO, 128), F32), vmem((4, 128, 1...  29 us
    pallas_call x1, Pallas kernels, per_device(): pl.pallas_call(last_kernel, out_shape=(pltpu.HBM((4, 128, LEV), F32), plt...  1.01 us

profile of v5, /device:TPU:1, one launch (start us, length us, event | category | flops | bytes accessed | tf_op | source)
XLA Modules:
  0.0 30.7 jit_solution(6202655746935725503)
XLA Ops:
  0.6 0.0 copy-start
  0.6 29.0 %physics_step.1 = (f32[112,128]{1,0:T(8,128)S(1)}, f32[4,128,128]{2,1,0:T(8,128)S(1)}, bf16[3,58,2048]{2,1,0:T(8,128)(2,1)S(1)}) custom-call(f32[4,128,72]{2,1,0:T(8,128)} %bitcast.7, bf16[3,58,2048]{2,1,0:T(8,128)(2,1)} %crm.1, s32[58,2048]{1,0:T(8,128)} %mask.1, s32[1,32]{1,0:T(1,128)} %bitcast.8, bf16[64,128]{1,0:T(8,128)(2,1)} %constant.14.clone.sums_in, ...), custom_call_target="tpu_custom_call" | custom-call | tf_op jit(solution)/shard_map/physics_step/pallas_call | solution.py:533
  29.7 0.0 copy-done
  29.7 1.0 %last_step.1 = (f32[4,128,72]{2,1,0:T(8,128)}, bf16[3,58,2048]{2,1,0:T(8,128)(2,1)}) custom-call(f32[112,128]{1,0:T(8,128)S(1)} %get-tuple-element.7.came_in, f32[4,128,128]{2,1,0:T(8,128)S(1)} %get-tuple-element.8.part, bf16[768,256]{1,0:T(8,128)(2,1)S(1)} %copy-done, bf16[3,58,2048]{2,1,0:T(8,128)(2,1)S(1)} %get-tuple-element.9.crm_in), custom_call_target="tpu_custom_call" | custom-call | tf_op jit(solution)/shard_map/last_step/pallas_call | solution.py:547
Async XLA Ops:
  0.6 29.0 %copy-start = (bf16[768,256]{1,0:T(8,128)(2,1)S(1)}, bf16[768,256]{1,0:T(8,128)(2,1)}, u32[]{:S(2)}) copy-start(bf16[768,256]{1,0:T(8,128)(2,1)} %constant.20.clone.arrive) | copy-start | bytes 1179652

commit v6 on v5

--- a/solution.py
+++ b/solution.py
@@ -336,11 +336,18 @@
 
     mine = lax.div(r, 2 * TILES)
 
-    def finish(group, own):
+    def finish(k, carry):
+        late = k >> 1
+        group = (3 - k) * (1 - late) + (k - 2) * late
         first = pl.multiple_of(group * TILES, TILES)
         near = ar.at[pl.ds(2 * first, 2 * TILES)]
-        due = ar.at[pl.ds(2 * first, 2 * TILES - own)]
-        pltpu.make_async_copy(due, due, tile_sem.at[group]).wait()
+
+        def wait(count):
+            due = ar.at[pl.ds(2 * first, count)]
+            pltpu.make_async_copy(due, due, tile_sem.at[group]).wait()
+
+        pl.when(group != mine)(lambda: wait(2 * TILES))
+        pl.when(group == mine)(lambda: wait(2 * TILES - 1))
         near = 0.3 * near[...].reshape(8 * TILES, 128)
         parts = [part.astype(F32) for part in (*halves(near), *halves(pltpu.roll(near, 64, 1)))]
         near = jnp.concatenate(
@@ -375,27 +382,21 @@
                 parts.append(halves(two[f]))
                 ob[f, :, at] = parts[f][0][0:CRM_LEV]
             change += [jnp.concatenate([part[h] for part in parts], axis=1) for h in range(2)]
-        mean = slot_means(means[...], jnp.concatenate(change, axis=0))
+        mean = [
+            slot_means(means[...], jnp.concatenate(change[2 * t : 2 * t + 2], axis=0))
+            for t in range(TILES)
+        ]
         for t in range(TILES):
-            part = mean[:, 128 * t : 128 * t + 128]
-            part = part + pltpu.roll(part, 64, 1)
+            part = mean[t] + pltpu.roll(mean[t], 64, 1)
             message = jnp.where(iota((8, 128), 1) < 64, part[0:8], part[8:16]) - xs[first + t]
             for pair in range(2):
                 rs[2 * (first + t) + pair] = message[4 * pair : 4 * pair + 4]
         for k in range(2 * TILES):
             target = 2 * first + k
-            if own:
-                pl.when(target != r)(tendency_copy(target).start)
-            else:
-                tendency_copy(target).start()
-
-    def others(k, carry):
-        away = (1 - 2 * (k & 1)) * ((k + 2) >> 1)
-        finish(lax.rem(mine + GROUPS + away, GROUPS), 0)
+            pl.when(target != r)(tendency_copy(target).start)
         return carry
 
-    lax.fori_loop(0, GROUPS - 1, others, None)
-    finish(mine, 1)
+    lax.fori_loop(0, GROUPS, finish, None)
     rt[r] = rs[r]
 
     store = pltpu.make_async_copy(ob, crm_out, store_sem.at[0])

time: 30.8 us -> 29.6 us (0.961)
  Pallas kernels: 30 us -> 28.8 us
    pallas_call x1, Pallas kernels: 29 us -> 27.8 us  [per_device(): pl.pallas_call(kernel, out_shape=(vmem((HALO, 128), F32), vmem((4, 128, 1...]
where the time goes in v6:
time: 29.6 us; the launch traced here: 29.4 us
  Pallas kernels  28.8 us (97%)
  between operations  0.65 us (2%)
    pallas_call x1, Pallas kernels, per_device(): pl.pallas_call(kernel, out_shape=(vmem((HALO, 128), F32), vmem((4, 128, 1...  27.8 us
    pallas_call x1, Pallas kernels, per_device(): pl.pallas_call(last_kernel, out_shape=(pltpu.HBM((4, 128, LEV), F32), plt...  1 us

profile of v6, /device:TPU:1, one launch (start us, length us, event | category | flops | bytes accessed | tf_op | source)
XLA Modules:
  0.0 29.4 jit_solution(14122717767898407013)
XLA Ops:
  0.6 0.0 copy-start
  0.6 27.8 %physics_step.1 = (f32[112,128]{1,0:T(8,128)S(1)}, f32[4,128,128]{2,1,0:T(8,128)S(1)}, bf16[3,58,2048]{2,1,0:T(8,128)(2,1)S(1)}) custom-call(f32[4,128,72]{2,1,0:T(8,128)} %bitcast.7, bf16[3,58,2048]{2,1,0:T(8,128)(2,1)} %crm.1, s32[58,2048]{1,0:T(8,128)} %mask.1, s32[1,32]{1,0:T(1,128)} %bitcast.8, bf16[64,128]{1,0:T(8,128)(2,1)} %constant.14.clone.sums_in, ...), custom_call_target="tpu_custom_call" | custom-call | tf_op jit(solution)/shard_map/physics_step/pallas_call | solution.py:534
  28.4 0.0 copy-done
  28.4 1.0 %last_step.1 = (f32[4,128,72]{2,1,0:T(8,128)}, bf16[3,58,2048]{2,1,0:T(8,128)(2,1)}) custom-call(f32[112,128]{1,0:T(8,128)S(1)} %get-tuple-element.7.came_in, f32[4,128,128]{2,1,0:T(8,128)S(1)} %get-tuple-element.8.part, bf16[768,256]{1,0:T(8,128)(2,1)S(1)} %copy-done, bf16[3,58,2048]{2,1,0:T(8,128)(2,1)S(1)} %get-tuple-element.9.crm_in), custom_call_target="tpu_custom_call" | custom-call | tf_op jit(solution)/shard_map/last_step/pallas_call | solution.py:548
Async XLA Ops:
  0.6 27.8 %copy-start = (bf16[768,256]{1,0:T(8,128)(2,1)S(1)}, bf16[768,256]{1,0:T(8,128)(2,1)}, u32[]{:S(2)}) copy-start(bf16[768,256]{1,0:T(8,128)(2,1)} %constant.20.clone.arrive) | copy-start | bytes 1179652

commit v7 on v6

--- a/solution.py
+++ b/solution.py
@@ -444,9 +444,10 @@
     lane = iota((128, 128), 1)
     given = [jnp.where(lane < CRM_LEV, value, 0.0) for value in (given, pltpu.roll(given, 64, 1))]
     given = jnp.concatenate(halves(jnp.concatenate(given, axis=0)), axis=1)
-    sent = dot(post[...], given)
-    sent = [sent[HALO * k : HALO * k + HALO] for k in range(4)]
-    sent = [sent[h][:, 0:128] + sent[h][:, 128:256] + sent[2 + h][:, 0:128] for h in range(2)]
+    sent = dot(post[0 : 2 * HALO, :], given)
+    low = dot(post[2 * HALO : 4 * HALO, :], given[:, 0:128])
+    sent = sent[:, 0:128] + sent[:, 128:256] + low
+    sent = [sent[0:HALO], sent[HALO:]]
     hs[...] = sent[0] + pltpu.roll(sent[1], 64, 1)
     for slot in (4, 5, 6, 7, 0, 1, 2, 3):
         at = pl.ds(CELL_AT[slot], CELL_ROWS[slot])

time: 29.6 us -> 29.5 us (level)
  no operation moved by 1% of the time
where the time goes in v7:
time: 29.5 us; the launch traced here: 29.4 us
  Pallas kernels  28.7 us (97%)
  between operations  0.65 us (2%)
    pallas_call x1, Pallas kernels, per_device(): pl.pallas_call(kernel, out_shape=(vmem((HALO, 128), F32), vmem((4, 128, 1...  27.7 us
    pallas_call x1, Pallas kernels, per_device(): pl.pallas_call(last_kernel, out_shape=(pltpu.HBM((4, 128, LEV), F32), plt...  1 us

profile of v7, /device:TPU:1, one launch (start us, length us, event | category | flops | bytes accessed | tf_op | source)
XLA Modules:
  0.0 29.4 jit_solution(16040849487013814607)
XLA Ops:
  0.6 0.0 copy-start
  0.6 27.7 %physics_step.1 = (f32[112,128]{1,0:T(8,128)S(1)}, f32[4,128,128]{2,1,0:T(8,128)S(1)}, bf16[3,58,2048]{2,1,0:T(8,128)(2,1)S(1)}) custom-call(f32[4,128,72]{2,1,0:T(8,128)} %bitcast.7, bf16[3,58,2048]{2,1,0:T(8,128)(2,1)} %crm.1, s32[58,2048]{1,0:T(8,128)} %mask.1, s32[1,32]{1,0:T(1,128)} %bitcast.8, bf16[64,128]{1,0:T(8,128)(2,1)} %constant.14.clone.sums_in, ...), custom_call_target="tpu_custom_call" | custom-call | tf_op jit(solution)/shard_map/physics_step/pallas_call | solution.py:535
  28.4 0.0 copy-done
  28.4 1.0 %last_step.1 = (f32[4,128,72]{2,1,0:T(8,128)}, bf16[3,58,2048]{2,1,0:T(8,128)(2,1)}) custom-call(f32[112,128]{1,0:T(8,128)S(1)} %get-tuple-element.7.came_in, f32[4,128,128]{2,1,0:T(8,128)S(1)} %get-tuple-element.8.part, bf16[768,256]{1,0:T(8,128)(2,1)S(1)} %copy-done, bf16[3,58,2048]{2,1,0:T(8,128)(2,1)S(1)} %get-tuple-element.9.crm_in), custom_call_target="tpu_custom_call" | custom-call | tf_op jit(solution)/shard_map/last_step/pallas_call | solution.py:549
Async XLA Ops:
  0.6 27.8 %copy-start = (bf16[768,256]{1,0:T(8,128)(2,1)S(1)}, bf16[768,256]{1,0:T(8,128)(2,1)}, u32[]{:S(2)}) copy-start(bf16[768,256]{1,0:T(8,128)(2,1)} %constant.20.clone.arrive) | copy-start | bytes 1179652
